TPU v7x, 256 devices: a whole 4x4x8 slice. The times are simulated.
256 devices in a mesh: sess: 32 (over x, z), hist: 8 (over y, core).
Axes of the slice: x: 4, y: 4, z: 8, core: 2. Of those that a mesh axis runs over, the one named last changes fastest.
Arguments:
- events: bfloat16 [8, 32, 512, 1024], P('hist', 'sess'), may hold values from -12 to 12
- w_qkv: bfloat16 [1024, 3072], replicated, may hold values from -0.1875 to 0.1875
- patterns: int32 [8, 32, 512], P('hist', 'sess'), may hold values from 0 to 31, never falling along the last dimension, each value on 1 to 48 neighbouring positions
- owners: int32 [8, 32, 32], P('hist', 'sess'), may hold values from 0 to 31, as said below
- gaps: int32 [8, 32, 32], P('hist', 'sess'), may hold values from 1 to 127
- rates: float32 [16], replicated, may hold values from 0.001171875 to 0.09375
- prior_state: float32 [32, 16, 64, 64], P('sess'), may hold values from -4 to 4
Outputs:
- user_out: float32 [8, 32, 32, 1024], P('hist', 'sess')
Inputs may be any that keep to these rules, and one draw needn't show every extreme that they name: `patterns`: every id of 0 to 31 occurs in each pack, ids never fall along a pack, each session has 1 to 48 events and one has exactly 48. `owners`: no user owns more than 2 sessions of one pack. In every history segment one user owns exactly 2 sessions of every pack of that segment.
All inputs are finite; a program needn't handle non-finite values.
Results may differ from a plain program's by a relative error of at most 0.0035.
Values sent between devices are 32-bit elements; how exact they have to be, the bound alone decides.
No kernel may reach another device: no remote copies, remote signals or barrier semaphores. Data moves between devices by JAX's collectives and lax.ppermute only.
A program may use at most 128 MiB of HBM per device.

v0:
```python
import jax
import jax.numpy as jnp
from jax import lax
from jax.sharding import PartitionSpec as P

HEADS = 16
SPP = 32


def entering(part, axis, combine, identity):
    place = lax.axis_index(axis)
    gathered = jax.tree.map(lambda a: lax.all_gather(a, axis), part)
    state = jax.tree.map(lambda a, e: jnp.zeros_like(a) + jnp.asarray(e, a.dtype), part, identity)

    def one(turn, state):
        return combine(
            state, jax.tree.map(lambda a: lax.dynamic_index_in_dim(a, turn, 0, False), gathered)
        )

    return lax.fori_loop(0, place, one, state)


def encode_pack(pack_events, pack_ids, w_qkv):
    length = pack_events.shape[0]
    width = w_qkv.shape[0]
    head_size = width // HEADS
    mixed = jnp.dot(pack_events, w_qkv, preferred_element_type=jnp.float32)
    query_b = mixed[:, :width].astype(jnp.bfloat16).reshape(length, HEADS, head_size)
    key_b = mixed[:, width : 2 * width].astype(jnp.bfloat16).reshape(length, HEADS, head_size)
    value_b = mixed[:, 2 * width :].astype(jnp.bfloat16).reshape(length, HEADS, head_size)
    scores = jnp.einsum(
        "qhd,khd->hqk", query_b, key_b, preferred_element_type=jnp.float32
    ) * head_size ** (-0.5)
    same_session = pack_ids[:, None] == pack_ids[None, :]
    scores = jnp.where(same_session[None], scores, -jnp.inf)
    peak = jnp.max(scores, axis=-1, keepdims=True)
    expd = jnp.exp(scores - peak)
    probs_b = (expd / jnp.sum(expd, axis=-1, keepdims=True)).astype(jnp.bfloat16)
    attended = jnp.einsum(
        "hqk,khd->qhd", probs_b, value_b, preferred_element_type=jnp.float32
    ).reshape(length, width)
    members = (pack_ids[None, :] == jnp.arange(SPP, dtype=jnp.int32)[:, None]).astype(jnp.float32)
    counts = jnp.sum(members, axis=1, keepdims=True)
    stacked = jnp.concatenate([attended, mixed[:, width:]], axis=1)
    return jnp.dot(members, stacked, precision=lax.Precision.HIGHEST) / counts


def combine_states(earlier, later):
    return (earlier[0] * later[0], later[0][:, None, None] * earlier[1] + later[1])


def shards(events, w_qkv, patterns, owners, gaps, rates, prior_state):
    sess_count = lax.axis_size("sess")
    packs = events.shape[1]
    width = w_qkv.shape[0]
    head_size = width // HEADS
    capacity = max(2, 2 * SPP // sess_count)
    per_source = packs * capacity
    total_slots = sess_count * per_source
    row_iota = lax.broadcasted_iota(jnp.int32, (SPP, SPP), 0)
    col_iota = lax.broadcasted_iota(jnp.int32, (SPP, SPP), 1)
    summary = encode_pack(events[0, 0], patterns[0, 0], w_qkv)
    fade_log = -rates[None, :] * gaps[0, 0][:, None].astype(jnp.float32)
    owner_row = owners[0, 0]
    same_owner = owner_row[:, None] == owner_row[None, :]
    ranks = jnp.sum(same_owner & (row_iota > col_iota), axis=1)
    slot_list = owner_row * per_source + 0 + ranks
    outgoing = jnp.zeros((total_slots, 3 * width), jnp.float32).at[slot_list].set(summary)
    outgoing_log = jnp.zeros((total_slots, HEADS), jnp.float32).at[slot_list].set(fade_log)
    arrived, arrived_log = (
        lax.all_to_all(
            outgoing.reshape(sess_count, per_source, 3 * width),
            "sess",
            split_axis=0,
            concat_axis=0,
            tiled=True,
        ),
        lax.all_to_all(
            outgoing_log.reshape(sess_count, per_source, HEADS),
            "sess",
            split_axis=0,
            concat_axis=0,
            tiled=True,
        ),
    )
    arrived = arrived.reshape(total_slots, 3 * width)
    arrived_log = arrived_log.reshape(total_slots, HEADS)
    query_rows = arrived[:, :width].reshape(total_slots, HEADS, head_size)
    key_portion = arrived[:, width : 2 * width].reshape(total_slots, HEADS, head_size)
    value_portion = arrived[:, 2 * width :].reshape(total_slots, HEADS, head_size)
    decay_sum = jnp.cumsum(arrived_log, axis=0)
    closing = decay_sum[-1]
    remaining_length = jnp.exp(closing[None, :] - decay_sum)
    segment_state = jnp.einsum(
        "vw,vwr,vwo->wro",
        remaining_length,
        key_portion,
        value_portion,
        precision=lax.Precision.HIGHEST,
    )
    segment_fade = jnp.exp(closing)
    start_fade = jnp.ones((HEADS,), jnp.float32)
    start_state = jnp.zeros_like(segment_state)
    before_fade, before_state = entering(
        (segment_fade, segment_state), "hist", combine_states, (start_fade, start_state)
    )
    incoming_state = before_fade[:, None, None] * prior_state[0] + before_state
    carried = jnp.exp(decay_sum)[:, :, None] * jnp.einsum(
        "olc,lcx->olx", query_rows, incoming_state, precision=lax.Precision.HIGHEST
    )
    log_gap = decay_sum[:, None, :] - decay_sum[None, :, :]
    lower = (
        lax.broadcasted_iota(jnp.int32, (total_slots, total_slots), 0)
        >= lax.broadcasted_iota(jnp.int32, (total_slots, total_slots), 1)
    )[:, :, None]
    weights = jnp.exp(jnp.where(lower, log_gap, -jnp.inf))
    local_scores = (
        jnp.einsum("thd,ihd->tih", query_rows, key_portion, precision=lax.Precision.HIGHEST)
        * weights
    )
    local = jnp.einsum("tih,ihe->the", local_scores, value_portion, precision=lax.Precision.HIGHEST)
    results = (carried + local).reshape(sess_count, per_source, width)
    returned = lax.all_to_all(results, "sess", split_axis=0, concat_axis=0, tiled=True).reshape(
        total_slots, width
    )
    picked = returned[slot_list]
    return picked.reshape(1, packs, SPP, width)


def solution(mesh):
    placed = (
        P("hist", "sess", None, None),
        P(),
        P("hist", "sess", None),
        P("hist", "sess", None),
        P("hist", "sess", None),
        P(),
        P("sess", None, None, None),
    )
    return jax.shard_map(
        shards, mesh=mesh, in_specs=placed, out_specs=P("hist", "sess", None, None), check_vma=False
    )
```

profile of v0, /device:TPU:57, one launch (start us, length us, event | category | flops | bytes accessed | tf_op | source)
XLA Modules:
  0.0 173.4 jit_solution(3922114450861586451)
XLA Ops:
  9.5 1.3 scatter_custom_fusion
  10.8 10.7 %all-to-all-start = ((f32[32,2,16]{2,1,0:T(2,128)}), f32[32,2,16]{2,1,0:T(2,128)}, u32[]{:S(2)}, u32[]{:S(2)}) async-start(f32[32,2,16]{2,1,0:T(2,128)} %bitcast.7), calls=%async_computation | async-start | bytes 65536 | tf_op jit(solution)/shard_map/all_to_all | solution.py:78
  23.2 5.5 %fusion.45 = (bf16[512,3072]{1,0:T(8,128)(2,1)S(1)}, f32[512,3072]{1,0:T(8,128)S(1)}) fusion(bf16[1024,3072]{1,0:T(8,128)(2,1)} %param.10, bf16[1,1,512,1024]{3,2,1,0:T(8,128)(2,1)S(1)} %copy-done), kind=kOutput, calls=%fused_computation.67 | convolution fusion | flops 3222798336 | bytes 16777216 | tf_op jit(solution)/shard_map/dot_general | solution.py:27
  28.8 2.4 %slice.41 = f32[512,2048]{1,0:T(8,128)} slice(f32[512,3072]{1,0:T(8,128)S(1)} %get-tuple-element.66), slice={[0:512], [1024:3072]} | slice | bytes 8388608 | tf_op jit(solution)/shard_map/slice | solution.py:44
  31.2 1.3 fusion.42
  32.5 2.3 %copy.70 = bf16[512,1024]{0,1:T(8,128)(2,1)} copy(bf16[512,1024]{1,0:T(8,128)(2,1)} %get-tuple-element.57) | data formatting | bytes 2097152 | tf_op jit(solution)/shard_map/slice | solution.py:30
  34.8 1.3 copy.71
  36.6 10.7 %fusion.46 = (f32[16,512]{1,0:T(8,128)S(1)}, f32[16,512,512]{1,2,0:T(8,128)}) fusion(pred[512,512]{0,1:T(8,128)(4,1)S(1)} %broadcast_compare_fusion, bf16[512,16,64]{0,2,1:T(8,128)(2,1)} %bitcast.71, bf16[512,16,64]{0,2,1:T(8,128)(2,1)S(1)} %bitcast.72), kind=kOutput, calls=%fused_computation.68 | convolution fusion | flops 553648640 | bytes 19169280 | tf_op jit(solution)/shard_map/sub | solution.py:37
  47.3 8.7 %fusion.5 = f32[16,64,512]{2,1,0:T(8,128)} fusion(bf16[512,16,64]{0,2,1:T(8,128)(2,1)S(1)} %bitcast.70, f32[16,512,512]{1,2,0:T(8,128)} %get-tuple-element.68, f32[16,512]{1,0:T(8,128)S(1)} %get-tuple-element.67), kind=kOutput, calls=%fused_computation.13 | convolution fusion | flops 545259520 | bytes 19955712 | tf_op jit(solution)/shard_map/hqk,khd->qhd/dot_general | solution.py:39
  56.0 1.9 %copy.74 = f32[512,1024]{1,0:T(8,128)S(1)} copy(f32[512,1024]{0,1:T(8,128)} %bitcast.68) | data formatting | bytes 4194304 | tf_op jit(solution)/shard_map/reshape | solution.py:41
  57.9 4.6 %fusion.10 = f32[32,3072]{1,0:T(8,128)S(1)} fusion(f32[512,2048]{1,0:T(8,128)} %slice.41, f32[512,1024]{1,0:T(8,128)S(1)} %copy.74, f32[32]{0:T(128)S(1)} %convert_reduce_fusion, s32[512]{0:T(512)S(1)} %bitcast.75), kind=kOutput, calls=%fused_computation.18 | convolution fusion | flops 605667328 | bytes 6686848 | tf_op jit(solution)/shard_map/dot_general | solution.py:45
  63.5 1.3 reshape.139
  64.9 9.2 %all-to-all-start.1 = ((f32[32,2,3072]{2,1,0:T(2,128)}), f32[32,2,3072]{2,1,0:T(2,128)S(1)}, u32[]{:S(2)}, u32[]{:S(2)}) async-start(f32[32,2,3072]{2,1,0:T(2,128)} %reshape.139), calls=%async_computation.1 | async-start | bytes 1572864 | tf_op jit(solution)/shard_map/all_to_all | solution.py:71
  75.2 19.5 %all-to-all-done.1 = f32[32,2,3072]{2,1,0:T(2,128)S(1)} async-done(((f32[32,2,3072]{2,1,0:T(2,128)}), f32[32,2,3072]{2,1,0:T(2,128)S(1)}, u32[]{:S(2)}, u32[]{:S(2)}) %all-to-all-start.1) | async-done | bytes 786464 | tf_op jit(solution)/shard_map/all_to_all | solution.py:71
  95.9 1.9 %fusion.23 = f32[16,64,64]{2,1,0:T(8,128)} fusion(f32[64,16,64]{0,2,1:T(8,128)S(1)} %bitcast.66, f32[64,16,64]{2,1,0:T(8,128)S(1)} %broadcast_multiply_fusion), kind=kOutput, calls=%fused_computation.31 | convolution fusion | flops 50331648 | bytes 786432 | tf_op jit(solution)/shard_map/vw,vwr,vwo->wro/dot_general | solution.py:94
  98.0 10.8 %all-gather.1 = f32[8,1,16]{2,1,0:T(1,128)S(1)} all-gather(f32[1,1,16]{2,1,0:T(1,128)S(1)} %get-tuple-element.64), channel_id=1, replica_groups=mesh['sess'=32,'hist'=8] {'hist'}, dimensions={0}, use_global_device_ids=true | all-gather | bytes 576 | tf_op jit(solution)/shard_map/all_gather | solution.py:12
  108.9 1.3 fusion.16
  110.2 20.1 %all-gather.4.cloned.1.call-done = f32[128,64,64]{2,1,0:T(8,128)} async-done(((f32[16,64,64]{2,1,0:T(8,128)}), f32[128,64,64]{2,1,0:T(8,128)}) %all-gather.4.cloned.1.call-update) | async-done | bytes 2097168 | tf_op jit(solution)/shard_map/all_gather | solution.py:12
  130.4 8.6 %while.12 = (s32[]{:T(128)}, f32[16]{0:T(128)S(1)}, f32[16,64,64]{2,1,0:T(8,128)S(1)}, s32[]{:T(128)}, f32[8,16]{1,0:T(8,128)S(1)}, /*index=5*/f32[8,16,64,64]{3,2,1,0:T(8,128)}, s32[]{:T(128)}, s32[]{:T(128)}, s32[]{:T(128)}) while((s32[]{:T(128)}, f32[16]{0:T(128)S(1)}, f32[16,64,64]{2,1,0:T(8,128)S(1)}, s32[]{:T(128)}, ...), condition=%wide.region_8.9_spmd, body=%wide.region_7.8_spmd.sunk | while | flops 131093 | bytes 786895 | solution.py:20
  130.4 1.2 bitcast_add_fusion.3
  139.0 2.2 %fusion.17 = f32[64,16,64]{0,2,1:T(8,128)S(1)} fusion(f32[16,64,64]{2,1,0:T(8,128)S(1)} %get-tuple-element.40, f32[1,16,64,64]{3,2,1,0:T(8,128)} %param.15, f32[64,16,64]{2,1,0:T(8,128)S(1)} %reshape.143, f32[16]{0:T(128)S(1)} %get-tuple-element.39, f32[64,16]{0,1:T(8,128)S(1)} %copy.69), kind=kOutput, calls=%fused_computation.25 | convolution fusion | flops 50528256 | bytes 1052736 | tf_op jit(solution)/shard_map/olc,lcx->olx/dot_general | solution.py:108
  143.1 9.5 %all-to-all-start.2 = ((f32[32,2,1024]{2,1,0:T(2,128)}), f32[32,2,1024]{2,1,0:T(2,128)S(1)}, u32[]{:S(2)}, u32[]{:S(2)}) async-start(f32[32,2,1024]{2,1,0:T(2,128)} %reshape.144), calls=%async_computation.2 | async-start | bytes 524288 | tf_op jit(solution)/shard_map/all_to_all | solution.py:123
  152.6 12.5 %all-to-all-done.2 = f32[32,2,1024]{2,1,0:T(2,128)S(1)} async-done(((f32[32,2,1024]{2,1,0:T(2,128)}), f32[32,2,1024]{2,1,0:T(2,128)S(1)}, u32[]{:S(2)}, u32[]{:S(2)}) %all-to-all-start.2) | async-done | bytes 262176 | tf_op jit(solution)/shard_map/all_to_all | solution.py:123
  165.3 1.3 gather_fusion
  (49 shorter events, 18.1 us)
Async XLA Ops:
  6.5 16.7 %copy-start = (bf16[1,1,512,1024]{3,2,1,0:T(8,128)(2,1)S(1)}, bf16[1,1,512,1024]{3,2,1,0:T(8,128)(2,1)}, u32[]{:S(2)}) copy-start(bf16[1,1,512,1024]{3,2,1,0:T(8,128)(2,1)} %param.9) | copy-start | bytes 3145732
  10.8 54.1 %all-to-all-start = ((f32[32,2,16]{2,1,0:T(2,128)}), f32[32,2,16]{2,1,0:T(2,128)}, u32[]{:S(2)}, u32[]{:S(2)}) async-start(f32[32,2,16]{2,1,0:T(2,128)} %bitcast.7), calls=%async_computation | async-start | bytes 65536 | tf_op jit(solution)/shard_map/all_to_all | solution.py:78
  36.6 10.7 %copy-start.1 = (bf16[512,1024]{0,1:T(8,128)(2,1)S(1)}, bf16[512,1024]{0,1:T(8,128)(2,1)}, u32[]{:S(2)}) copy-start(bf16[512,1024]{0,1:T(8,128)(2,1)} %copy.70) | copy-start | bytes 3145732
  47.3 10.6 %copy-start.2 = (s32[1,1,512]{2,1,0:T(1,128)S(1)}, s32[1,1,512]{2,1,0:T(1,128)}, u32[]{:S(2)}) copy-start(s32[1,1,512]{2,1,0:T(1,128)} %param.11) | copy-start | bytes 6148
  64.9 29.9 %all-to-all-start.1 = ((f32[32,2,3072]{2,1,0:T(2,128)}), f32[32,2,3072]{2,1,0:T(2,128)S(1)}, u32[]{:S(2)}, u32[]{:S(2)}) async-start(f32[32,2,3072]{2,1,0:T(2,128)} %reshape.139), calls=%async_computation.1 | async-start | bytes 1572864 | tf_op jit(solution)/shard_map/all_to_all | solution.py:71
  74.1 56.2 %all-gather.4.cloned.1.call-start = ((), (), s32[]{:S(2)}) async-start(), calls=%async_computation.3 | async-start | bytes 4718592 | tf_op jit(solution)/shard_map/all_gather | solution.py:12
  143.1 22.0 %all-to-all-start.2 = ((f32[32,2,1024]{2,1,0:T(2,128)}), f32[32,2,1024]{2,1,0:T(2,128)S(1)}, u32[]{:S(2)}, u32[]{:S(2)}) async-start(f32[32,2,1024]{2,1,0:T(2,128)} %reshape.144), calls=%async_computation.2 | async-start | bytes 524288 | tf_op jit(solution)/shard_map/all_to_all | solution.py:123
Sparse Core Ops, SparseCore 0:
  98.0 32.3 all-gather.3
where the time goes:
time: 174 us; the launch traced here: 173 us
  waiting for transfers between devices  52.2 us (30%)
  matrix products  35.4 us (20%)
  starting transfers between devices  29.6 us (17%)
  local copies, waits for them, and re-layouts  16.1 us (9%)
  other arithmetic  15.5 us (9%)
  between operations  13.6 us (8%)
  blocking collectives  10.8 us (6%)
    all_gather x1, waiting for transfers between devices, entering(): gathered = jax.tree.map(lambda a: lax.all_gather(a, axis), part)  20.1 us
    all_to_all x1, waiting for transfers between devices, shards(): lax.all_to_all(outgoing.reshape(sess_count, per_source, 3 * width), 'sess...  19.5 us
    all_to_all x1, waiting for transfers between devices, shards(): lax.all_to_all(results, 'sess', split_axis=0, concat_axis=0, tiled=True)  12.5 us
    all_gather x1, blocking collectives, entering(): gathered = jax.tree.map(lambda a: lax.all_gather(a, axis), part)  10.8 us
    all_to_all x1, starting transfers between devices, shards(): lax.all_to_all(outgoing_log.reshape(sess_count, per_source, HEADS), 'sess...  10.7 us
    sub x1, matrix products, encode_pack(): expd = jnp.exp(scores - peak)  10.7 us
    all_to_all x1, starting transfers between devices, shards(): lax.all_to_all(results, 'sess', split_axis=0, concat_axis=0, tiled=True)  9.49 us
    all_to_all x1, starting transfers between devices, shards(): lax.all_to_all(outgoing.reshape(sess_count, per_source, 3 * width), 'sess...  9.22 us
  transfers between devices with their start and end apart: 4, of which 3 were waited for; matrix products, arithmetic and copies ran while one was open for 26% of the time, Pallas kernels for 0%

commit v1 on v0

v1 whole, which is shorter than its diff:
```python
import functools

import jax
import jax.numpy as jnp
from jax import lax
from jax.experimental import pallas as pl
from jax.experimental.pallas import tpu as pltpu
from jax.sharding import PartitionSpec as P

HEADS = 16
SPP = 32
LONGEST = 48
HALO = 64
QUERIES = 128
PARTS = 7
BF16 = jnp.bfloat16
F32 = jnp.float32
NT = (((1,), (1,)), ((), ()))
TN = (((0,), (0,)), ((), ()))


def iota(shape, dim):
    return lax.broadcasted_iota(jnp.int32, shape, dim)


def mm(a, b, dims=(((1,), (0,)), ((), ()))):
    return lax.dot_general(a, b, dims, preferred_element_type=F32)


def split(x):
    high = x.astype(BF16)
    return high, (x - high.astype(F32)).astype(BF16)


def mm3(a, b, dims=(((1,), (0,)), ((), ()))):
    a_high, a_low = split(a)
    b_high, b_low = split(b)
    return mm(a_high, b_high, dims) + (mm(a_low, b_high, dims) + mm(a_high, b_low, dims))


def slots_of(owner_row, users):
    owned = owner_row == iota((users, SPP), 0)
    earlier = (iota((SPP, SPP), 0) < iota((SPP, SPP), 1)).astype(BF16)
    before = mm(owned.astype(F32).astype(BF16), earlier)
    return [(owned & (before == float(rank))).astype(F32) for rank in range(2)]


def windows(length):
    result = []
    for start in range(0, length, QUERIES):
        low, high = max(0, start - HALO), min(length, start + QUERIES + HALO)
        result.append((start, low, high - low))
    return result


def encode_kernel(
    users,
    groups,
    events_ref,
    wq_ref,
    wk_ref,
    wv_ref,
    pattern_ref,
    owner_ref,
    gap_ref,
    out_ref,
    mask_ref,
    place_ref,
    inverse_ref,
    weight_ref,
):
    step = pl.program_id(0)
    length = events_ref.shape[0]
    columns = wq_ref.shape[1]
    here = columns // 64

    @pl.when(step == 0)
    def _():
        pattern = pattern_ref[...]
        members = (pattern == iota((SPP, length), 0)).astype(F32).astype(BF16)
        slots = slots_of(owner_ref[...], users)
        place = mm(jnp.concatenate(slots, axis=0).astype(BF16), members)
        place_ref[...] = place.astype(BF16)
        counts = jnp.sum(place, axis=1, keepdims=True)
        inverse_ref[...] = jnp.broadcast_to(1.0 / jnp.maximum(counts, 1.0), inverse_ref.shape)
        ids = iota((SPP, QUERIES), 0).astype(F32).astype(BF16)
        id_column = mm(members, ids, TN)
        id_row = pattern.astype(F32)
        offset = 0
        for start, low, size in windows(length):
            same = id_column[low : low + size] == id_row[:, start : start + QUERIES]
            mask_ref[offset : offset + size, :] = jnp.where(same, 0.0, -jnp.inf)
            offset += size
        gap_row = gap_ref[...].astype(F32)
        gap_columns = [jnp.sum(slot * gap_row, axis=1, keepdims=True) for slot in slots]
        both = jnp.where(iota((users, 128), 1) < 64, gap_columns[0], gap_columns[1])
        for group in range(groups):
            out_ref[pl.ds(group * users * PARTS + 6, users, stride=PARTS), :] = both

    events = events_ref[...]
    query = mm(events, wq_ref[...]).astype(BF16)
    key = mm(events, wk_ref[...])
    value = mm(events, wv_ref[...])
    key_b = key.astype(BF16)
    head_of = iota((1, columns), 1) // 64
    only = [jnp.where(head_of == head, 0.125, 0.0).astype(BF16) for head in range(here)]
    spread = (
        (iota((here * QUERIES, columns), 0) // QUERIES == iota((here * QUERIES, columns), 1) // 64)
        .astype(F32)
        .astype(BF16)
    )
    weight_ref[...] = jnp.zeros_like(weight_ref)
    offset = 0
    for start, low, size in windows(length):
        block = query[start : start + QUERIES]
        stacked = jnp.concatenate([block * keep for keep in only], axis=0)
        scores = mm(key_b[low : low + size], stacked, NT)
        mask = mask_ref[offset : offset + size, :]
        offset += size
        probs = []
        for head in range(here):
            part = scores[:, head * QUERIES : (head + 1) * QUERIES] + mask
            expd = jnp.exp(part - jnp.max(part, axis=0, keepdims=True))
            probs.append((expd * (1.0 / jnp.sum(expd, axis=0, keepdims=True))).astype(BF16))
        weight_ref[low : low + size, :] += mm(jnp.concatenate(probs, axis=1), spread)
    weighted = weight_ref[...] * value.astype(BF16).astype(F32)
    place = place_ref[...]
    inverse = inverse_ref[...]
    for part, rows in enumerate((weighted, key, value)):
        high, low = split(rows)
        means = mm(place, high) + mm(place, low)
        for sub in range(columns // 128):
            group = step * (columns // 128) + sub
            for rank in range(2):
                out_ref[pl.ds(group * users * PARTS + part * 2 + rank, users, stride=PARTS), :] = (
                    means[rank * users : (rank + 1) * users, sub * 128 : (sub + 1) * 128]
                    * inverse[rank * users : (rank + 1) * users]
                )


def encode(events, w_qkv, patterns, owners, gaps, users, groups):
    length, width = events.shape
    columns = 256
    steps = width // columns
    window_rows = sum(size for _, _, size in windows(length))
    rows = groups * users * PARTS
    whole = lambda shape: pl.BlockSpec(shape, lambda i: (0, 0))
    column = lambda part: pl.BlockSpec((width, columns), lambda i: (0, part * steps + i))
    return pl.pallas_call(
        functools.partial(encode_kernel, users, groups),
        grid=(steps,),
        in_specs=[
            whole((length, width)),
            column(0),
            column(1),
            column(2),
            whole((1, length)),
            whole((1, SPP)),
            whole((1, SPP)),
        ],
        out_specs=whole((rows, 128)),
        out_shape=jax.ShapeDtypeStruct((rows, 128), F32),
        scratch_shapes=[
            pltpu.VMEM((window_rows, QUERIES), F32),
            pltpu.VMEM((2 * users, length), BF16),
            pltpu.VMEM((2 * users, 128), F32),
            pltpu.VMEM((length, columns), F32),
        ],
        compiler_params=pltpu.CompilerParams(vmem_limit_bytes=40 * 1024 * 1024),
        name="encode",
    )(events, w_qkv, w_qkv, w_qkv, patterns, owners, gaps)


def recur_kernel(packs, group_ref, rates_ref, rows_ref, prior_ref, out_ref):
    group = group_ref[0]
    rate = [rates_ref[2 * group], rates_ref[2 * group + 1]]
    rows = 2 * packs
    load = lambda part: rows_ref[pl.ds(part, packs, stride=PARTS), :]
    both = lambda part: jnp.concatenate([load(part), load(part + 1)], axis=0)
    query, key, value = both(0), both(2), both(4)
    first = iota((rows, 128), 1) < 64
    gap = load(6)
    turned = pltpu.roll(gap, 64, 1)
    gap = jnp.concatenate(
        [jnp.where(first[:packs], gap, turned), jnp.where(first[:packs], turned, gap)], axis=0
    ).astype(BF16)
    time = lambda dim: (
        lambda n: jnp.where(n >= packs, 2 * (n - packs) + 1, 2 * n)
    )(iota((rows, rows), dim))
    causal = time(0) >= time(1)
    elapsed = mm(causal.astype(F32).astype(BF16), gap)
    elapsed_row = elapsed.T[0:1, :]
    since = jnp.where(causal, elapsed[:, 0:1] - elapsed_row, 1e30)
    key_high, key_low = split(key)
    value_high, value_low = split(value)
    result = None
    for head in range(2):
        mine = first if head == 0 else jnp.logical_not(first)
        q_high, q_low = split(jnp.where(mine, query, 0.0))
        scores = mm(q_high, key_high, NT) + (mm(q_low, key_high, NT) + mm(q_high, key_low, NT))
        scores = scores * jnp.exp(-rate[head] * since)
        s_high, s_low = split(scores)
        local = mm(s_high, value_high) + (mm(s_low, value_high) + mm(s_high, value_low))
        result = local if head == 0 else jnp.where(first, result, local)
    lane_rate = jnp.where(first, rate[0], rate[1])
    faded = query * jnp.exp(-lane_rate * elapsed)
    empty = jnp.zeros((64, 64), F32)
    prior = jnp.concatenate(
        [
            jnp.concatenate([prior_ref[0], empty], axis=1),
            jnp.concatenate([empty, prior_ref[1]], axis=1),
        ],
        axis=0,
    )
    result = result + mm3(faded, prior)
    for rank in range(2):
        out_ref[pl.ds(rank, packs, stride=2), :] = result[rank * packs : (rank + 1) * packs]


def recur(group, rates, rows, prior, packs):
    return pl.pallas_call(
        functools.partial(recur_kernel, packs),
        grid_spec=pltpu.PrefetchScalarGridSpec(
            num_scalar_prefetch=2,
            grid=(1,),
            in_specs=[
                pl.BlockSpec(rows.shape, lambda i, group, rates: (0, 0)),
                pl.BlockSpec((2, 64, 64), lambda i, group, rates: (group[0], 0, 0)),
            ],
            out_specs=pl.BlockSpec((2 * packs, 128), lambda i, group, rates: (0, 0)),
        ),
        out_shape=jax.ShapeDtypeStruct((2 * packs, 128), F32),
        compiler_params=pltpu.CompilerParams(vmem_limit_bytes=40 * 1024 * 1024),
        name="recur",
    )(group, rates, rows, prior)


def pick_kernel(users, groups, owner_ref, rows_ref, out_ref):
    slots = jnp.concatenate(slots_of(owner_ref[...], users), axis=0).astype(BF16)
    for group in range(groups):
        mine = jnp.concatenate(
            [rows_ref[pl.ds(group * users * 2 + rank, users, stride=2), :] for rank in range(2)],
            axis=0,
        )
        high = mine.astype(BF16)
        rest = mine - high.astype(F32)
        middle, low = split(rest)
        out_ref[:, group * 128 : (group + 1) * 128] = mm(slots, high, TN) + (
            mm(slots, middle, TN) + mm(slots, low, TN)
        )


def pick(owners, rows, users, groups):
    return pl.pallas_call(
        functools.partial(pick_kernel, users, groups),
        out_shape=jax.ShapeDtypeStruct((SPP, groups * 128), F32),
        compiler_params=pltpu.CompilerParams(vmem_limit_bytes=16 * 1024 * 1024),
        name="pick",
    )(owners, rows)


def shards(events, w_qkv, patterns, owners, gaps, rates, prior_state):
    groups = lax.axis_size("hist")
    users = lax.axis_size("sess")
    packs = groups * users
    axes = ("hist", "sess")
    send = encode(events[0, 0], w_qkv, patterns[0], owners[0], gaps[0], users, groups)
    arrived = lax.all_to_all(
        send.reshape(packs, PARTS, 1, 128), axes, split_axis=0, concat_axis=0, tiled=True
    ).reshape(packs * PARTS, 128)
    group = lax.axis_index("hist").astype(jnp.int32).reshape(1)
    done = recur(group, rates, arrived, prior_state[0], packs)
    returned = lax.all_to_all(
        done.reshape(packs, 2, 128), axes, split_axis=0, concat_axis=0, tiled=True
    ).reshape(packs * 2, 128)
    return pick(owners[0], returned, users, groups)[None, None]


def solution(mesh):
    placed = (
        P("hist", "sess", None, None),
        P(),
        P("hist", "sess", None),
        P("hist", "sess", None),
        P("hist", "sess", None),
        P(),
        P("sess", None, None, None),
    )
    return jax.shard_map(
        shards, mesh=mesh, in_specs=placed, out_specs=P("hist", "sess", None, None), check_vma=False
    )
```

time: 174 us -> 89.3 us (0.51)
  the two profiles are of different devices: /device:TPU:57 before, /device:TPU:1 now
where the time goes in v1:
time: 89.3 us; the launch traced here: 89.1 us
  waiting for transfers between devices  29.6 us (33%)
  blocking collectives  20.9 us (23%)
  Pallas kernels  16.9 us (19%)
  starting transfers between devices  15.7 us (18%)
  local copies, waits for them, and re-layouts  6.01 us (7%)
    all_to_all x1, waiting for transfers between devices, shards(): lax.all_to_all(send.reshape(packs, PARTS, 1, 128), axes, split_axis=0, co...  29.6 us
    all_to_all x1, blocking collectives, shards(): lax.all_to_all(done.reshape(packs, 2, 128), axes, split_axis=0, concat_ax...  20.9 us
    all_to_all x1, starting transfers between devices, shards(): lax.all_to_all(send.reshape(packs, PARTS, 1, 128), axes, split_axis=0, co...  15.7 us
    pallas_call x1, Pallas kernels, encode(): pl.pallas_call(functools.partial(encode_kernel, users, groups), grid=(ste...  12.8 us
    unnamed x16, local copies, waits for them, and re-layouts  6.01 us
    pallas_call x1, Pallas kernels, recur(): pl.pallas_call(functools.partial(recur_kernel, packs), grid_spec=pltpu.Pr...  3.12 us
  transfers between devices with their start and end apart: 1, of which 1 were waited for; matrix products, arithmetic and copies ran while one was open for 0% of the time, Pallas kernels for 0%

profile of v1, /device:TPU:1, one launch (start us, length us, event | category | flops | bytes accessed | tf_op | source)
XLA Modules:
  0.0 89.1 jit_solution(1049406165211943528)
XLA Ops:
  0.0 0.0 copy-start
  0.0 2.8 %copy-done = bf16[1024,3072]{1,0:T(8,128)(2,1)S(1)} copy-done((bf16[1024,3072]{1,0:T(8,128)(2,1)S(1)}, bf16[1024,3072]{1,0:T(8,128)(2,1)}, u32[]{:S(2)}) %copy-start) | copy-done | bytes 6291480
  2.8 0.0 copy-start.1
  2.8 1.2 %copy-done.1 = bf16[1,1,512,1024]{3,2,1,0:T(8,128)(2,1)S(1)} copy-done((bf16[1,1,512,1024]{3,2,1,0:T(8,128)(2,1)S(1)}, bf16[1,1,512,1024]{3,2,1,0:T(8,128)(2,1)}, u32[]{:S(2)}) %copy-start.1) | copy-done | bytes 1048600
  4.0 0.0 copy-start.3
  4.0 0.7 copy-done.3
  4.7 0.0 copy-start.4
  4.7 0.7 copy-done.4
  5.3 0.0 copy-start.6
  5.4 0.7 copy-done.6
  6.0 0.0 copy-start.2
  6.0 0.0 copy-start.7
  6.0 0.0 copy-start.5
  6.0 12.8 %encode.1 = f32[1792,128]{1,0:T(8,128)} custom-call(bf16[512,1024]{1,0:T(8,128)(2,1)S(1)} %bitcast.12, bf16[1024,3072]{1,0:T(8,128)(2,1)S(1)} %copy-done, bf16[1024,3072]{1,0:T(8,128)(2,1)S(1)} %copy-done, bf16[1024,3072]{1,0:T(8,128)(2,1)S(1)} %copy-done, s32[1,512]{1,0:T(1,128)S(1)} %bitcast.16, s32[1,32]{1,0:T(1,128)S(1)} %bitcast.17, s32[1,32]{1,0:T(1,128)S(1)} %bitcast.19), custom_call_target="tpu_custom_call" | custom-call | tf_op jit(solution)/shard_map/encode/pallas_call | solution.py:149
  18.8 15.7 %all-to-all-start = ((f32[256,7,1,128]{3,2,1,0:T(1,128)}), f32[256,7,1,128]{3,2,1,0:T(1,128)S(1)}, u32[]{:S(2)}, u32[]{:S(2)}) async-start(f32[256,7,1,128]{3,2,1,0:T(1,128)} %bitcast.5), calls=%async_computation | async-start | bytes 1835008 | tf_op jit(solution)/shard_map/all_to_all | solution.py:268
  34.4 29.6 %all-to-all-done = f32[256,7,1,128]{3,2,1,0:T(1,128)S(1)} async-done(((f32[256,7,1,128]{3,2,1,0:T(1,128)}), f32[256,7,1,128]{3,2,1,0:T(1,128)S(1)}, u32[]{:S(2)}, u32[]{:S(2)}) %all-to-all-start) | async-done | bytes 917536 | tf_op jit(solution)/shard_map/all_to_all | solution.py:268
  64.0 0.0 copy-done.2
  64.0 0.0 copy-done.7
  64.0 3.1 %recur.1 = f32[512,128]{1,0:T(8,128)S(1)} custom-call(s32[1]{0:T(128)} %bitcast.1.group_ref, f32[16]{0:T(128)S(1)} %copy-done.7, f32[1792,128]{1,0:T(8,128)S(1)} %bitcast.11, f32[16,64,64]{2,1,0:T(8,128)S(1)} %bitcast.15), custom_call_target="tpu_custom_call" | custom-call | tf_op jit(solution)/shard_map/recur/pallas_call | solution.py:221
  67.1 20.9 %all_to_all.10 = f32[256,2,128]{2,1,0:T(2,128)S(1)} all-to-all(f32[256,2,128]{2,1,0:T(2,128)S(1)} %bitcast.14), channel_id=1, replica_groups=mesh['sess'=32,'hist'=8] {'hist','sess'}, dimensions={0} | all-to-all | bytes 524288 | tf_op jit(solution)/shard_map/all_to_all | solution.py:273
  88.0 0.0 copy-done.5
  88.0 1.1 %pick.1 = f32[32,1024]{1,0:T(8,128)} custom-call(s32[1,32]{1,0:T(1,128)S(1)} %bitcast.18, f32[512,128]{1,0:T(8,128)S(1)} %bitcast.13), custom_call_target="tpu_custom_call" | custom-call | tf_op jit(solution)/shard_map/pick/pallas_call | solution.py:254
Async XLA Ops:
  0.0 2.8 %copy-start = (bf16[1024,3072]{1,0:T(8,128)(2,1)S(1)}, bf16[1024,3072]{1,0:T(8,128)(2,1)}, u32[]{:S(2)}) copy-start(bf16[1024,3072]{1,0:T(8,128)(2,1)} %wv_ref.1) | copy-start | bytes 18874372
  2.8 1.2 %copy-start.1 = (bf16[1,1,512,1024]{3,2,1,0:T(8,128)(2,1)S(1)}, bf16[1,1,512,1024]{3,2,1,0:T(8,128)(2,1)}, u32[]{:S(2)}) copy-start(bf16[1,1,512,1024]{3,2,1,0:T(8,128)(2,1)} %param.7) | copy-start | bytes 3145732
  4.0 0.7 copy-start.3
  4.7 0.7 copy-start.4
  5.3 0.7 copy-start.6
  6.0 58.0 %copy-start.2 = (f32[1,16,64,64]{3,2,1,0:T(8,128)S(1)}, f32[1,16,64,64]{3,2,1,0:T(8,128)}, u32[]{:S(2)}) copy-start(f32[1,16,64,64]{3,2,1,0:T(8,128)} %param.13) | copy-start | bytes 786436
  6.0 58.0 %copy-start.7 = (f32[16]{0:T(128)S(1)}, f32[16]{0:T(128)}, u32[]{:S(2)}) copy-start(f32[16]{0:T(128)} %rates_ref.1) | copy-start | bytes 196
  6.0 82.0 %copy-start.5 = (s32[1,1,32]{2,1,0:T(1,128)S(1)}, s32[1,1,32]{2,1,0:T(1,128)}, u32[]{:S(2)}) copy-start(s32[1,1,32]{2,1,0:T(1,128)} %param.10) | copy-start | bytes 388
  18.8 45.2 %all-to-all-start = ((f32[256,7,1,128]{3,2,1,0:T(1,128)}), f32[256,7,1,128]{3,2,1,0:T(1,128)S(1)}, u32[]{:S(2)}, u32[]{:S(2)}) async-start(f32[256,7,1,128]{3,2,1,0:T(1,128)} %bitcast.5), calls=%async_computation | async-start | bytes 1835008 | tf_op jit(solution)/shard_map/all_to_all | solution.py:268

commit v2 on v1

--- a/solution.py
+++ b/solution.py
@@ -10,8 +10,7 @@
 HEADS = 16
 SPP = 32
 LONGEST = 48
-HALO = 64
-QUERIES = 128
+QUERIES = 64
 PARTS = 7
 BF16 = jnp.bfloat16
 F32 = jnp.float32
@@ -48,7 +47,7 @@
 def windows(length):
     result = []
     for start in range(0, length, QUERIES):
-        low, high = max(0, start - HALO), min(length, start + QUERIES + HALO)
+        low, high = max(0, start - LONGEST), min(length, start + QUERIES + LONGEST)
         result.append((start, low, high - low))
     return result
 
@@ -56,86 +55,143 @@
 def encode_kernel(
     users,
     groups,
-    events_ref,
-    wq_ref,
-    wk_ref,
-    wv_ref,
+    events_hbm,
+    w_hbm,
+    pattern_hbm,
+    owner_hbm,
+    gap_hbm,
+    out_ref,
+    rows_ref,
+    w_ref,
     pattern_ref,
     owner_ref,
     gap_ref,
-    out_ref,
     mask_ref,
-    place_ref,
-    inverse_ref,
+    query_ref,
+    key_ref,
+    value_ref,
     weight_ref,
+    small_sem,
+    events_sem,
+    w_sem,
 ):
-    step = pl.program_id(0)
-    length = events_ref.shape[0]
-    columns = wq_ref.shape[1]
+    length, width = events_hbm.shape
+    columns = 256
     here = columns // 64
-
-    @pl.when(step == 0)
-    def _():
-        pattern = pattern_ref[...]
-        members = (pattern == iota((SPP, length), 0)).astype(F32).astype(BF16)
-        slots = slots_of(owner_ref[...], users)
-        place = mm(jnp.concatenate(slots, axis=0).astype(BF16), members)
-        place_ref[...] = place.astype(BF16)
-        counts = jnp.sum(place, axis=1, keepdims=True)
-        inverse_ref[...] = jnp.broadcast_to(1.0 / jnp.maximum(counts, 1.0), inverse_ref.shape)
-        ids = iota((SPP, QUERIES), 0).astype(F32).astype(BF16)
-        id_column = mm(members, ids, TN)
-        id_row = pattern.astype(F32)
-        offset = 0
-        for start, low, size in windows(length):
-            same = id_column[low : low + size] == id_row[:, start : start + QUERIES]
-            mask_ref[offset : offset + size, :] = jnp.where(same, 0.0, -jnp.inf)
-            offset += size
-        gap_row = gap_ref[...].astype(F32)
-        gap_columns = [jnp.sum(slot * gap_row, axis=1, keepdims=True) for slot in slots]
-        both = jnp.where(iota((users, 128), 1) < 64, gap_columns[0], gap_columns[1])
-        for group in range(groups):
-            out_ref[pl.ds(group * users * PARTS + 6, users, stride=PARTS), :] = both
-
-    events = events_ref[...]
-    query = mm(events, wq_ref[...]).astype(BF16)
-    key = mm(events, wk_ref[...])
-    value = mm(events, wv_ref[...])
-    key_b = key.astype(BF16)
+    steps = width // columns
+    small = [
+        pltpu.make_async_copy(source, target, small_sem.at[n])
+        for n, (source, target) in enumerate(
+            [(pattern_hbm, pattern_ref), (owner_hbm, owner_ref), (gap_hbm, gap_ref)]
+        )
+    ]
+    in_events = pltpu.make_async_copy(events_hbm, rows_ref.at[0:length], events_sem)
+    in_w = [
+        [
+            pltpu.make_async_copy(
+                w_hbm.at[:, part * width + step * columns : part * width + (step + 1) * columns],
+                w_ref.at[step * 3 + part],
+                w_sem.at[step * 3 + part],
+            )
+            for part in range(3)
+        ]
+        for step in range(steps)
+    ]
+    for copy in small:
+        copy.start()
+    in_events.start()
+    for copies in in_w:
+        for copy in copies:
+            copy.start()
+    for copy in small:
+        copy.wait()
+
+    pattern = pattern_ref[...]
+    members = (pattern == iota((SPP, length), 0)).astype(F32).astype(BF16)
+    slots = slots_of(owner_ref[...], users)
+    place = mm(jnp.concatenate(slots, axis=0).astype(BF16), members)
+    counts = jnp.sum(place, axis=1, keepdims=True)
+    place = place.astype(BF16)
+    inverse = jnp.broadcast_to(1.0 / jnp.maximum(counts, 1.0), (2 * users, columns))
+    ids = iota((SPP, 128), 0).astype(F32).astype(BF16)
+    id_column = mm(members, ids, TN)
+    id_row = pattern.astype(F32)
+    offset = 0
+    for start, low, size in windows(length):
+        block = id_row[:, start : start + QUERIES]
+        same = id_column[low : low + size] == jnp.concatenate([block, block], axis=1)
+        mask_ref[offset : offset + size, :] = jnp.where(same, 0.0, -jnp.inf)
+        offset += size
+    gap_row = gap_ref[...].astype(F32)
+    gap_columns = [jnp.sum(slot * gap_row, axis=1, keepdims=True) for slot in slots]
+    both = jnp.where(iota((users, 128), 1) < 64, gap_columns[0], gap_columns[1])
+    for group in range(groups):
+        out_ref[pl.ds(group * users * PARTS + 6, users, stride=PARTS), :] = both
+
     head_of = iota((1, columns), 1) // 64
     only = [jnp.where(head_of == head, 0.125, 0.0).astype(BF16) for head in range(here)]
     spread = (
-        (iota((here * QUERIES, columns), 0) // QUERIES == iota((here * QUERIES, columns), 1) // 64)
+        (iota((columns, columns), 0) // QUERIES == iota((columns, columns), 1) // 64)
         .astype(F32)
         .astype(BF16)
     )
-    weight_ref[...] = jnp.zeros_like(weight_ref)
-    offset = 0
-    for start, low, size in windows(length):
-        block = query[start : start + QUERIES]
-        stacked = jnp.concatenate([block * keep for keep in only], axis=0)
-        scores = mm(key_b[low : low + size], stacked, NT)
-        mask = mask_ref[offset : offset + size, :]
-        offset += size
-        probs = []
-        for head in range(here):
-            part = scores[:, head * QUERIES : (head + 1) * QUERIES] + mask
-            expd = jnp.exp(part - jnp.max(part, axis=0, keepdims=True))
-            probs.append((expd * (1.0 / jnp.sum(expd, axis=0, keepdims=True))).astype(BF16))
-        weight_ref[low : low + size, :] += mm(jnp.concatenate(probs, axis=1), spread)
-    weighted = weight_ref[...] * value.astype(BF16).astype(F32)
-    place = place_ref[...]
-    inverse = inverse_ref[...]
-    for part, rows in enumerate((weighted, key, value)):
-        high, low = split(rows)
-        means = mm(place, high) + mm(place, low)
+
+    in_events.wait()
+    high, low = split(mm(place, rows_ref[0:length, :]))
+    rows_ref[length : length + 2 * users, :] = high
+    rows_ref[length + 2 * users :, :] = low
+
+    def store(step, part, means):
         for sub in range(columns // 128):
             group = step * (columns // 128) + sub
             for rank in range(2):
-                out_ref[pl.ds(group * users * PARTS + part * 2 + rank, users, stride=PARTS), :] = (
-                    means[rank * users : (rank + 1) * users, sub * 128 : (sub + 1) * 128]
-                    * inverse[rank * users : (rank + 1) * users]
-                )
+                out_ref[
+                    pl.ds(group * users * PARTS + part * 2 + rank, users, stride=PARTS), :
+                ] = means[rank * users : (rank + 1) * users, sub * 128 : (sub + 1) * 128]
+
+    def project(step):
+        query_ref[step] = mm(rows_ref[0:length, :], w_ref[step * 3]).astype(BF16)
+        for part, target in ((1, key_ref), (2, value_ref)):
+            mixed = mm(rows_ref[...], w_ref[step * 3 + part])
+            means = mixed[length : length + 2 * users] + mixed[length + 2 * users :]
+            store(step, part, means * inverse)
+            target[step] = mixed[:length].astype(BF16)
+
+    def attend(step):
+        offset = 0
+        reached = 0
+        for start, low, size in windows(length):
+            block = query_ref[step, start : start + QUERIES, :]
+            stacked = jnp.concatenate([block * keep for keep in only], axis=0)
+            scores = mm(key_ref[step, low : low + size, :], stacked, NT)
+            mask = mask_ref[offset : offset + size, :]
+            offset += size
+            probs = []
+            for half in range(columns // 128):
+                part = scores[:, half * 128 : (half + 1) * 128] + mask
+                expd = jnp.exp(part - jnp.max(part, axis=0, keepdims=True))
+                probs.append(expd * (1.0 / jnp.sum(expd, axis=0, keepdims=True)))
+            probs = jnp.concatenate(probs, axis=1)
+            known = reached - low
+            if known:
+                weight_ref[step, low:reached, :] += probs[:known]
+            weight_ref[step, reached : low + size, :] = probs[known:]
+            reached = low + size
+
+    def finish(step):
+        weight = mm(weight_ref[step].astype(BF16), spread)
+        high, low = split(weight * value_ref[step].astype(F32))
+        store(step, 0, (mm(place, high) + mm(place, low)) * inverse)
+
+    for copies in in_w:
+        for copy in copies:
+            copy.wait()
+    for step in range(steps):
+        project(step)
+    for step in range(steps):
+        attend(step)
+    for step in range(steps):
+        finish(step)
 
 
 def encode(events, w_qkv, patterns, owners, gaps, users, groups):
@@ -144,31 +200,28 @@
     steps = width // columns
     window_rows = sum(size for _, _, size in windows(length))
     rows = groups * users * PARTS
-    whole = lambda shape: pl.BlockSpec(shape, lambda i: (0, 0))
-    column = lambda part: pl.BlockSpec((width, columns), lambda i: (0, part * steps + i))
     return pl.pallas_call(
         functools.partial(encode_kernel, users, groups),
-        grid=(steps,),
-        in_specs=[
-            whole((length, width)),
-            column(0),
-            column(1),
-            column(2),
-            whole((1, length)),
-            whole((1, SPP)),
-            whole((1, SPP)),
-        ],
-        out_specs=whole((rows, 128)),
+        in_specs=[pl.BlockSpec(memory_space=pl.ANY)] * 5,
         out_shape=jax.ShapeDtypeStruct((rows, 128), F32),
         scratch_shapes=[
-            pltpu.VMEM((window_rows, QUERIES), F32),
-            pltpu.VMEM((2 * users, length), BF16),
-            pltpu.VMEM((2 * users, 128), F32),
-            pltpu.VMEM((length, columns), F32),
+            pltpu.VMEM((length + 4 * users, width), BF16),
+            pltpu.VMEM((3 * steps, width, columns), BF16),
+            pltpu.VMEM((1, length), jnp.int32),
+            pltpu.VMEM((1, SPP), jnp.int32),
+            pltpu.VMEM((1, SPP), jnp.int32),
+            pltpu.VMEM((window_rows, 128), F32),
+            pltpu.VMEM((steps, length, columns), BF16),
+            pltpu.VMEM((steps, length, columns), BF16),
+            pltpu.VMEM((steps, length, columns), BF16),
+            pltpu.VMEM((steps, length, columns), F32),
+            pltpu.SemaphoreType.DMA((3,)),
+            pltpu.SemaphoreType.DMA,
+            pltpu.SemaphoreType.DMA((3 * steps,)),
         ],
-        compiler_params=pltpu.CompilerParams(vmem_limit_bytes=40 * 1024 * 1024),
+        compiler_params=pltpu.CompilerParams(vmem_limit_bytes=60 * 1024 * 1024),
         name="encode",
-    )(events, w_qkv, w_qkv, w_qkv, patterns, owners, gaps)
+    )(events, w_qkv, patterns, owners, gaps)
 
 
 def recur_kernel(packs, group_ref, rates_ref, rows_ref, prior_ref, out_ref):

time: 89.3 us -> 81.4 us (0.912)
  local copies, waits for them, and re-layouts: 6.01 us -> 0.01 us
  Pallas kernels: 16.9 us -> 15.1 us
    unnamed x16 -> x6, local copies, waits for them, and re-layouts: 6.01 us -> 0.01 us
    pallas_call x1, Pallas kernels: 12.8 us -> 11 us  [encode(): pl.pallas_call(functools.partial(encode_kernel, users, groups), in_specs=...]
where the time goes in v2:
time: 81.4 us; the launch traced here: 81.2 us
  waiting for transfers between devices  29.6 us (36%)
  blocking collectives  20.8 us (26%)
  starting transfers between devices  15.7 us (19%)
  Pallas kernels  15.1 us (19%)
    all_to_all x1, waiting for transfers between devices, shards(): lax.all_to_all(send.reshape(packs, PARTS, 1, 128), axes, split_axis=0, co...  29.6 us
    all_to_all x1, blocking collectives, shards(): lax.all_to_all(done.reshape(packs, 2, 128), axes, split_axis=0, concat_ax...  20.8 us
    all_to_all x1, starting transfers between devices, shards(): lax.all_to_all(send.reshape(packs, PARTS, 1, 128), axes, split_axis=0, co...  15.7 us
    pallas_call x1, Pallas kernels, encode(): pl.pallas_call(functools.partial(encode_kernel, users, groups), in_specs=...  11 us
    pallas_call x1, Pallas kernels, recur(): pl.pallas_call(functools.partial(recur_kernel, packs), grid_spec=pltpu.Pr...  3.12 us
  transfers between devices with their start and end apart: 1, of which 1 were waited for; matrix products, arithmetic and copies ran while one was open for 0% of the time, Pallas kernels for 0%

profile of v2, /device:TPU:1, one launch (start us, length us, event | category | flops | bytes accessed | tf_op | source)
XLA Modules:
  0.0 81.2 jit_solution(15076964315128198893)
XLA Ops:
  0.0 0.0 copy-start.1
  0.0 0.0 copy-start
  0.0 0.0 copy-start.2
  0.0 11.0 %encode.1 = f32[1792,128]{1,0:T(8,128)} custom-call(bf16[512,1024]{1,0:T(8,128)(2,1)} %bitcast.18, bf16[1024,3072]{1,0:T(8,128)(2,1)} %w_hbm.1, s32[1,512]{1,0:T(1,128)} %bitcast.19, s32[1,32]{1,0:T(1,128)} %bitcast.15, s32[1,32]{1,0:T(1,128)} %bitcast.20), custom_call_target="tpu_custom_call" | custom-call | tf_op jit(solution)/shard_map/encode/pallas_call | solution.py:203
  11.0 15.7 %all-to-all-start = ((f32[256,7,1,128]{3,2,1,0:T(1,128)}), f32[256,7,1,128]{3,2,1,0:T(1,128)S(1)}, u32[]{:S(2)}, u32[]{:S(2)}) async-start(f32[256,7,1,128]{3,2,1,0:T(1,128)} %bitcast.17), calls=%async_computation | async-start | bytes 1835008 | tf_op jit(solution)/shard_map/all_to_all | solution.py:321
  26.7 29.6 %all-to-all-done = f32[256,7,1,128]{3,2,1,0:T(1,128)S(1)} async-done(((f32[256,7,1,128]{3,2,1,0:T(1,128)}), f32[256,7,1,128]{3,2,1,0:T(1,128)S(1)}, u32[]{:S(2)}, u32[]{:S(2)}) %all-to-all-start) | async-done | bytes 917536 | tf_op jit(solution)/shard_map/all_to_all | solution.py:321
  56.2 0.0 copy-done
  56.2 0.0 copy-done.2
  56.2 3.1 %recur.1 = f32[512,128]{1,0:T(8,128)S(1)} custom-call(s32[1]{0:T(128)} %bitcast.1.group_ref, f32[16]{0:T(128)S(1)} %copy-done.2, f32[1792,128]{1,0:T(8,128)S(1)} %bitcast.11, f32[16,64,64]{2,1,0:T(8,128)S(1)} %bitcast.14), custom_call_target="tpu_custom_call" | custom-call | tf_op jit(solution)/shard_map/recur/pallas_call | solution.py:274
  59.4 20.8 %all_to_all.10 = f32[256,2,128]{2,1,0:T(2,128)S(1)} all-to-all(f32[256,2,128]{2,1,0:T(2,128)S(1)} %bitcast.13), channel_id=1, replica_groups=mesh['sess'=32,'hist'=8] {'hist','sess'}, dimensions={0} | all-to-all | bytes 524288 | tf_op jit(solution)/shard_map/all_to_all | solution.py:326
  80.2 0.0 copy-done.1
  80.2 1.1 %pick.1 = f32[32,1024]{1,0:T(8,128)} custom-call(s32[1,32]{1,0:T(1,128)S(1)} %bitcast.16, f32[512,128]{1,0:T(8,128)S(1)} %bitcast.12), custom_call_target="tpu_custom_call" | custom-call | tf_op jit(solution)/shard_map/pick/pallas_call | solution.py:307
Async XLA Ops:
  0.0 80.2 %copy-start.1 = (s32[1,1,32]{2,1,0:T(1,128)S(1)}, s32[1,1,32]{2,1,0:T(1,128)}, u32[]{:S(2)}) copy-start(s32[1,1,32]{2,1,0:T(1,128)} %param.10) | copy-start | bytes 388
  0.0 56.2 %copy-start = (f32[1,16,64,64]{3,2,1,0:T(8,128)S(1)}, f32[1,16,64,64]{3,2,1,0:T(8,128)}, u32[]{:S(2)}) copy-start(f32[1,16,64,64]{3,2,1,0:T(8,128)} %param.13) | copy-start | bytes 786436
  0.0 56.2 %copy-start.2 = (f32[16]{0:T(128)S(1)}, f32[16]{0:T(128)}, u32[]{:S(2)}) copy-start(f32[16]{0:T(128)} %rates_ref.1) | copy-start | bytes 196
  11.0 45.2 %all-to-all-start = ((f32[256,7,1,128]{3,2,1,0:T(1,128)}), f32[256,7,1,128]{3,2,1,0:T(1,128)S(1)}, u32[]{:S(2)}, u32[]{:S(2)}) async-start(f32[256,7,1,128]{3,2,1,0:T(1,128)} %bitcast.17), calls=%async_computation | async-start | bytes 1835008 | tf_op jit(solution)/shard_map/all_to_all | solution.py:321

commit v3 on v2

--- a/solution.py
+++ b/solution.py
@@ -100,9 +100,8 @@
     for copy in small:
         copy.start()
     in_events.start()
-    for copies in in_w:
-        for copy in copies:
-            copy.start()
+    for copy in in_w[0]:
+        copy.start()
     for copy in small:
         copy.wait()
 
@@ -137,6 +136,9 @@
     )
 
     in_events.wait()
+    for copies in in_w[1:]:
+        for copy in copies:
+            copy.start()
     high, low = split(mm(place, rows_ref[0:length, :]))
     rows_ref[length : length + 2 * users, :] = high
     rows_ref[length + 2 * users :, :] = low
@@ -150,12 +152,15 @@
                 ] = means[rank * users : (rank + 1) * users, sub * 128 : (sub + 1) * 128]
 
     def project(step):
-        query_ref[step] = mm(rows_ref[0:length, :], w_ref[step * 3]).astype(BF16)
+        for at in range(0, length, 256):
+            chunk = rows_ref[at : at + 256, :]
+            query_ref[step, at : at + 256, :] = mm(chunk, w_ref[step * 3]).astype(BF16)
         for part, target in ((1, key_ref), (2, value_ref)):
-            mixed = mm(rows_ref[...], w_ref[step * 3 + part])
-            means = mixed[length : length + 2 * users] + mixed[length + 2 * users :]
-            store(step, part, means * inverse)
-            target[step] = mixed[:length].astype(BF16)
+            for at in range(0, length, 256):
+                chunk = rows_ref[at : at + 256, :]
+                target[step, at : at + 256, :] = mm(chunk, w_ref[step * 3 + part]).astype(BF16)
+            extra = mm(rows_ref[length:, :], w_ref[step * 3 + part])
+            store(step, part, (extra[: 2 * users] + extra[2 * users :]) * inverse)
 
     def attend(step):
         offset = 0
@@ -183,15 +188,23 @@
         high, low = split(weight * value_ref[step].astype(F32))
         store(step, 0, (mm(place, high) + mm(place, low)) * inverse)
 
-    for copies in in_w:
+    for copy in in_w[0]:
+        copy.wait()
+    project(0)
+    for copies in in_w[1:]:
         for copy in copies:
             copy.wait()
-    for step in range(steps):
-        project(step)
-    for step in range(steps):
-        attend(step)
-    for step in range(steps):
-        finish(step)
+    project(1)
+    project(2)
+    project(3)
+    attend(0)
+    attend(1)
+    attend(2)
+    finish(0)
+    finish(1)
+    attend(3)
+    finish(2)
+    finish(3)
 
 
 def encode(events, w_qkv, patterns, owners, gaps, users, groups):
@@ -224,39 +237,54 @@
     )(events, w_qkv, patterns, owners, gaps)
 
 
-def recur_kernel(packs, group_ref, rates_ref, rows_ref, prior_ref, out_ref):
-    group = group_ref[0]
+def recur_kernel(packs, rates_hbm, rows_ref, prior_hbm, out_ref, rates_ref, prior_ref, sem):
+    group = lax.axis_index("hist")
+    in_rates = pltpu.make_async_copy(rates_hbm, rates_ref, sem.at[0])
+    in_prior = pltpu.make_async_copy(prior_hbm.at[pl.ds(2 * group, 2)], prior_ref, sem.at[1])
+    in_rates.start()
+    in_prior.start()
+    half = packs // 2
+    rows = 2 * packs
+    load = lambda part, late: rows_ref[pl.ds(late * half * PARTS + part, half, stride=PARTS), :]
+    both = lambda part: jnp.concatenate(
+        [load(part + rank, late) for late in range(2) for rank in range(2)], axis=0
+    )
+    first = iota((1, 128), 1) < 64
+
+    def time(dim):
+        n = iota((rows, rows), dim)
+        return 2 * (n // packs * half + n % half) + n % packs // half
+
+    gap = []
+    for late in range(2):
+        stored = load(6, late)
+        turned = pltpu.roll(stored, 64, 1)
+        gap += [jnp.where(first, stored, turned), jnp.where(first, turned, stored)]
+    causal = time(0) >= time(1)
+    elapsed = mm(causal.astype(F32).astype(BF16), jnp.concatenate(gap, axis=0).astype(BF16))
+    since = jnp.where(causal, elapsed[:, 0:1] - elapsed.T[0:1, :], 1e30)
+
+    query, key, value = both(0), both(2), both(4)
+    turned_query, turned_key = pltpu.roll(query, 64, 1), pltpu.roll(key, 64, 1)
+    value_high, value_low = split(value)
+    value_both = jnp.concatenate([value_high, value_low], axis=1)
+    in_rates.wait()
+    in_prior.wait()
     rate = [rates_ref[2 * group], rates_ref[2 * group + 1]]
-    rows = 2 * packs
-    load = lambda part: rows_ref[pl.ds(part, packs, stride=PARTS), :]
-    both = lambda part: jnp.concatenate([load(part), load(part + 1)], axis=0)
-    query, key, value = both(0), both(2), both(4)
-    first = iota((rows, 128), 1) < 64
-    gap = load(6)
-    turned = pltpu.roll(gap, 64, 1)
-    gap = jnp.concatenate(
-        [jnp.where(first[:packs], gap, turned), jnp.where(first[:packs], turned, gap)], axis=0
-    ).astype(BF16)
-    time = lambda dim: (
-        lambda n: jnp.where(n >= packs, 2 * (n - packs) + 1, 2 * n)
-    )(iota((rows, rows), dim))
-    causal = time(0) >= time(1)
-    elapsed = mm(causal.astype(F32).astype(BF16), gap)
-    elapsed_row = elapsed.T[0:1, :]
-    since = jnp.where(causal, elapsed[:, 0:1] - elapsed_row, 1e30)
-    key_high, key_low = split(key)
-    value_high, value_low = split(value)
-    result = None
+
+    def pieces(x):
+        high = x.astype(BF16).astype(F32)
+        return high, x - high
+
+    sides = []
     for head in range(2):
         mine = first if head == 0 else jnp.logical_not(first)
-        q_high, q_low = split(jnp.where(mine, query, 0.0))
-        scores = mm(q_high, key_high, NT) + (mm(q_low, key_high, NT) + mm(q_high, key_low, NT))
-        scores = scores * jnp.exp(-rate[head] * since)
-        s_high, s_low = split(scores)
-        local = mm(s_high, value_high) + (mm(s_low, value_high) + mm(s_high, value_low))
-        result = local if head == 0 else jnp.where(first, result, local)
-    lane_rate = jnp.where(first, rate[0], rate[1])
-    faded = query * jnp.exp(-lane_rate * elapsed)
+        q_high, q_low = pieces(jnp.where(mine, query, turned_query))
+        k_high, k_low = pieces(jnp.where(mine, key, turned_key))
+        left = jnp.concatenate([jnp.where(first, q_high, q_low), jnp.where(first, q_high, 0.0)], axis=1)
+        right = jnp.concatenate([k_high, jnp.where(first, k_low, 0.0)], axis=1)
+        sides.append((left.astype(BF16), right.astype(BF16)))
+
     empty = jnp.zeros((64, 64), F32)
     prior = jnp.concatenate(
         [
@@ -265,48 +293,77 @@
         ],
         axis=0,
     )
-    result = result + mm3(faded, prior)
-    for rank in range(2):
-        out_ref[pl.ds(rank, packs, stride=2), :] = result[rank * packs : (rank + 1) * packs]
-
-
-def recur(group, rates, rows, prior, packs):
+    prior_high, prior_low = split(prior)
+    prior_twice = jnp.concatenate([prior_high, prior_high], axis=0)
+    lane_rate = jnp.where(first, rate[0], rate[1])
+
+    for late in range(2):
+        mine = slice(late * packs, (late + 1) * packs)
+        seen = slice(0, (late + 1) * packs)
+        heads = []
+        for head in range(2):
+            left, right = sides[head]
+            scores = mm(left[mine], right[seen], NT) * jnp.exp(-rate[head] * since[mine, seen])
+            s_high, s_low = split(scores)
+            wide = mm(s_high, value_both[seen])
+            heads.append(wide[:, :128] + (wide[:, 128:] + mm(s_low, value_high[seen])))
+        f_high, f_low = split(query[mine] * jnp.exp(-lane_rate * elapsed[mine]))
+        carried = mm(jnp.concatenate([f_high, f_low], axis=1), prior_twice) + mm(f_high, prior_low)
+        result = jnp.where(first, heads[0], heads[1]) + carried
+        for rank in range(2):
+            out_ref[pl.ds(late * packs + rank, half, stride=2), :] = (
+                result[rank * half : (rank + 1) * half]
+            )
+
+
+def recur(rates, rows, prior, packs):
     return pl.pallas_call(
         functools.partial(recur_kernel, packs),
-        grid_spec=pltpu.PrefetchScalarGridSpec(
-            num_scalar_prefetch=2,
-            grid=(1,),
-            in_specs=[
-                pl.BlockSpec(rows.shape, lambda i, group, rates: (0, 0)),
-                pl.BlockSpec((2, 64, 64), lambda i, group, rates: (group[0], 0, 0)),
-            ],
-            out_specs=pl.BlockSpec((2 * packs, 128), lambda i, group, rates: (0, 0)),
-        ),
+        in_specs=[
+            pl.BlockSpec(memory_space=pl.ANY),
+            pl.BlockSpec(memory_space=pltpu.VMEM),
+            pl.BlockSpec(memory_space=pl.ANY),
+        ],
         out_shape=jax.ShapeDtypeStruct((2 * packs, 128), F32),
+        scratch_shapes=[
+            pltpu.SMEM(rates.shape, F32),
+            pltpu.VMEM((2, 64, 64), F32),
+            pltpu.SemaphoreType.DMA((2,)),
+        ],
         compiler_params=pltpu.CompilerParams(vmem_limit_bytes=40 * 1024 * 1024),
         name="recur",
-    )(group, rates, rows, prior)
-
-
-def pick_kernel(users, groups, owner_ref, rows_ref, out_ref):
+    )(rates, rows, prior)
+
+
+def pick_kernel(users, groups, owner_hbm, rows_ref, out_ref, owner_ref, sem):
+    in_owner = pltpu.make_async_copy(owner_hbm, owner_ref, sem)
+    in_owner.start()
+    in_owner.wait()
     slots = jnp.concatenate(slots_of(owner_ref[...], users), axis=0).astype(BF16)
-    for group in range(groups):
-        mine = jnp.concatenate(
-            [rows_ref[pl.ds(group * users * 2 + rank, users, stride=2), :] for rank in range(2)],
-            axis=0,
-        )
-        high = mine.astype(BF16)
-        rest = mine - high.astype(F32)
-        middle, low = split(rest)
-        out_ref[:, group * 128 : (group + 1) * 128] = mm(slots, high, TN) + (
-            mm(slots, middle, TN) + mm(slots, low, TN)
-        )
+    mine = jnp.concatenate(
+        [
+            jnp.concatenate(
+                [rows_ref[pl.ds(group * users * 2 + rank, users, stride=2), :] for rank in range(2)],
+                axis=0,
+            )
+            for group in range(groups)
+        ],
+        axis=1,
+    )
+    high = mine.astype(BF16)
+    middle, low = split(mine - high.astype(F32))
+    out_ref[...] = mm(slots, high, TN) + (mm(slots, middle, TN) + mm(slots, low, TN))
 
 
 def pick(owners, rows, users, groups):
     return pl.pallas_call(
         functools.partial(pick_kernel, users, groups),
+        in_specs=[
+            pl.BlockSpec(memory_space=pl.ANY),
+            pl.BlockSpec(memory_space=pltpu.VMEM),
+        ],
         out_shape=jax.ShapeDtypeStruct((SPP, groups * 128), F32),
+        scratch_shapes=[pltpu.VMEM((1, SPP), jnp.int32), pltpu.SemaphoreType.DMA],
         compiler_params=pltpu.CompilerParams(vmem_limit_bytes=16 * 1024 * 1024),
         name="pick",
     )(owners, rows)
@@ -321,8 +378,7 @@
     arrived = lax.all_to_all(
         send.reshape(packs, PARTS, 1, 128), axes, split_axis=0, concat_axis=0, tiled=True
     ).reshape(packs * PARTS, 128)
-    group = lax.axis_index("hist").astype(jnp.int32).reshape(1)
-    done = recur(group, rates, arrived, prior_state[0], packs)
+    done = recur(rates, arrived, prior_state[0], packs)
     returned = lax.all_to_all(
         done.reshape(packs, 2, 128), axes, split_axis=0, concat_axis=0, tiled=True
     ).reshape(packs * 2, 128)

time: 81.4 us -> 79.9 us (0.982)
  blocking collectives: 20.8 us -> 66.1 us
  waiting for transfers between devices: 29.6 us -> 0 us
  starting transfers between devices: 15.7 us -> 0 us
  Pallas kernels: 15.1 us -> 13.6 us
    all_to_all x0 -> x1, blocking collectives: none -> 45.2 us  [shards(): lax.all_to_all(send.reshape(packs, PARTS, 1, 128), axes, split_axis=0, co...]
    all_to_all x1 -> x0, waiting for transfers between devices: 29.6 us -> none  [shards(): lax.all_to_all(send.reshape(packs, PARTS, 1, 128), axes, split_axis=0, co...]
    all_to_all x1 -> x0, starting transfers between devices: 15.7 us -> none  [shards(): lax.all_to_all(send.reshape(packs, PARTS, 1, 128), axes, split_axis=0, co...]
    pallas_call x2, Pallas kernels: 4.18 us -> 3.13 us  [the longest x1 2.1 us: recur(): pl.pallas_call(functools.partial(recur_kernel, packs), in_specs=[pl.Block...]
  transfers between devices with their start and end apart: 1 -> 0, of which waited for: 1 -> 0; matrix products, arithmetic and copies ran while one was open for 0% -> 0% of each run, Pallas kernels for 0% -> 0%
where the time goes in v3:
time: 79.9 us; the launch traced here: 79.8 us
  blocking collectives  66.1 us (83%)
  Pallas kernels  13.6 us (17%)
    all_to_all x1, blocking collectives, shards(): lax.all_to_all(send.reshape(packs, PARTS, 1, 128), axes, split_axis=0, co...  45.2 us
    all_to_all x1, blocking collectives, shards(): lax.all_to_all(done.reshape(packs, 2, 128), axes, split_axis=0, concat_ax...  20.8 us
    pallas_call x1, Pallas kernels, encode(): pl.pallas_call(functools.partial(encode_kernel, users, groups), in_specs=...  10.5 us
    pallas_call x1, Pallas kernels, recur(): pl.pallas_call(functools.partial(recur_kernel, packs), in_specs=[pl.Block...  2.1 us

profile of v3, /device:TPU:1, one launch (start us, length us, event | category | flops | bytes accessed | tf_op | source)
XLA Modules:
  0.0 79.8 jit_solution(18264148116154186977)
XLA Ops:
  0.0 0.0 copy-start.1
  0.0 0.0 copy-start
  0.0 0.0 copy-start.2
  0.0 10.5 %encode.1 = f32[1792,128]{1,0:T(8,128)} custom-call(bf16[512,1024]{1,0:T(8,128)(2,1)} %bitcast.17, bf16[1024,3072]{1,0:T(8,128)(2,1)} %w_hbm.1, s32[1,512]{1,0:T(1,128)} %bitcast.18, s32[1,32]{1,0:T(1,128)} %bitcast.14, s32[1,32]{1,0:T(1,128)} %bitcast.19), custom_call_target="tpu_custom_call" | custom-call | tf_op jit(solution)/shard_map/encode/pallas_call | solution.py:216
  10.5 45.2 %all_to_all.10 = f32[256,7,1,128]{3,2,1,0:T(1,128)S(1)} all-to-all(f32[256,7,1,128]{3,2,1,0:T(1,128)} %bitcast.16), channel_id=1, replica_groups=mesh['sess'=32,'hist'=8] {'hist','sess'}, dimensions={0} | all-to-all | bytes 1835008 | tf_op jit(solution)/shard_map/all_to_all | solution.py:378
  55.8 0.0 copy-done
  55.8 0.0 copy-done.2
  55.8 2.1 %recur.1 = f32[512,128]{1,0:T(8,128)S(1)} custom-call(f32[16]{0:T(128)S(1)} %copy-done.2, f32[1792,128]{1,0:T(8,128)S(1)} %bitcast.10, f32[16,64,64]{2,1,0:T(8,128)S(1)} %bitcast.13), custom_call_target="tpu_custom_call" | custom-call | tf_op jit(solution)/shard_map/recur/pallas_call | solution.py:320
  57.9 20.8 %all_to_all.11 = f32[256,2,128]{2,1,0:T(2,128)S(1)} all-to-all(f32[256,2,128]{2,1,0:T(2,128)S(1)} %bitcast.11), channel_id=1, replica_groups=mesh['sess'=32,'hist'=8] {'hist','sess'}, dimensions={0} | all-to-all | bytes 524288 | tf_op jit(solution)/shard_map/all_to_all | solution.py:382
  78.7 0.0 copy-done.1
  78.7 1.0 %pick.1 = f32[32,1024]{1,0:T(8,128)} custom-call(s32[1,32]{1,0:T(1,128)S(1)} %bitcast.15, f32[512,128]{1,0:T(8,128)S(1)} %bitcast.12), custom_call_target="tpu_custom_call" | custom-call | tf_op jit(solution)/shard_map/pick/pallas_call | solution.py:359
Async XLA Ops:
  0.0 78.7 %copy-start.1 = (s32[1,1,32]{2,1,0:T(1,128)S(1)}, s32[1,1,32]{2,1,0:T(1,128)}, u32[]{:S(2)}) copy-start(s32[1,1,32]{2,1,0:T(1,128)} %param.10) | copy-start | bytes 388
  0.0 55.8 %copy-start = (f32[1,16,64,64]{3,2,1,0:T(8,128)S(1)}, f32[1,16,64,64]{3,2,1,0:T(8,128)}, u32[]{:S(2)}) copy-start(f32[1,16,64,64]{3,2,1,0:T(8,128)} %param.13) | copy-start | bytes 786436
  0.0 55.8 %copy-start.2 = (f32[16]{0:T(128)S(1)}, f32[16]{0:T(128)}, u32[]{:S(2)}) copy-start(f32[16]{0:T(128)} %rates_hbm.1) | copy-start | bytes 196

commit v4 on v3

--- a/solution.py
+++ b/solution.py
@@ -11,7 +11,7 @@
 SPP = 32
 LONGEST = 48
 QUERIES = 64
-PARTS = 7
+PARTS = 6
 BF16 = jnp.bfloat16
 F32 = jnp.float32
 NT = (((1,), (1,)), ((), ()))
@@ -35,6 +35,11 @@
     a_high, a_low = split(a)
     b_high, b_low = split(b)
     return mm(a_high, b_high, dims) + (mm(a_low, b_high, dims) + mm(a_high, b_low, dims))
+
+
+def same_head(columns):
+    shape = (columns, columns)
+    return (iota(shape, 0) // 64 == iota(shape, 1) // 64).astype(F32).astype(BF16)
 
 
 def slots_of(owner_row, users):
@@ -60,12 +65,18 @@
     pattern_hbm,
     owner_hbm,
     gap_hbm,
-    out_ref,
+    rates_hbm,
+    send_hbm,
+    keep_hbm,
+    send_ref,
+    keep_ref,
+    fade_ref,
     rows_ref,
     w_ref,
     pattern_ref,
     owner_ref,
     gap_ref,
+    rates_ref,
     mask_ref,
     query_ref,
     key_ref,
@@ -74,15 +85,23 @@
     small_sem,
     events_sem,
     w_sem,
+    out_sem,
 ):
     length, width = events_hbm.shape
     columns = 256
     here = columns // 64
     steps = width // columns
+    subs = columns // 128
+    chunk = subs * users * PARTS
     small = [
         pltpu.make_async_copy(source, target, small_sem.at[n])
         for n, (source, target) in enumerate(
-            [(pattern_hbm, pattern_ref), (owner_hbm, owner_ref), (gap_hbm, gap_ref)]
+            [
+                (pattern_hbm, pattern_ref),
+                (owner_hbm, owner_ref),
+                (gap_hbm, gap_ref),
+                (rates_hbm, rates_ref),
+            ]
         )
     ]
     in_events = pltpu.make_async_copy(events_hbm, rows_ref.at[0:length], events_sem)
@@ -95,6 +114,20 @@
             )
             for part in range(3)
         ]
+        for step in range(steps)
+    ]
+    out_keys = pltpu.make_async_copy(
+        keep_ref.at[2 * users :], keep_hbm.at[2 * users :], out_sem.at[steps]
+    )
+    out_queries = pltpu.make_async_copy(
+        keep_ref.at[0 : 2 * users], keep_hbm.at[0 : 2 * users], out_sem.at[steps + 1]
+    )
+    out = [
+        pltpu.make_async_copy(
+            send_ref.at[step * chunk : (step + 1) * chunk],
+            send_hbm.at[step * chunk : (step + 1) * chunk],
+            out_sem.at[step],
+        )
         for step in range(steps)
     ]
     for copy in small:
@@ -122,45 +155,65 @@
         mask_ref[offset : offset + size, :] = jnp.where(same, 0.0, -jnp.inf)
         offset += size
     gap_row = gap_ref[...].astype(F32)
-    gap_columns = [jnp.sum(slot * gap_row, axis=1, keepdims=True) for slot in slots]
-    both = jnp.where(iota((users, 128), 1) < 64, gap_columns[0], gap_columns[1])
+    gaps = [jnp.sum(slot * gap_row, axis=1, keepdims=True) for slot in slots]
+    lane = iota((1, 128), 1)
+    first = lane < 64
     for group in range(groups):
-        out_ref[pl.ds(group * users * PARTS + 6, users, stride=PARTS), :] = both
+        at = slice(group * 128, (group + 1) * 128)
+        rate = jnp.where(first, rates_ref[2 * group], rates_ref[2 * group + 1])
+        fade_ref[0:users, at] = jnp.exp(-rate * gaps[0])
+        fade_ref[users:, at] = jnp.exp(-rate * (gaps[0] + gaps[1]))
+        keep_ref[6 * users :, at] = jnp.exp(-rate * gaps[1])
 
     head_of = iota((1, columns), 1) // 64
     only = [jnp.where(head_of == head, 0.125, 0.0).astype(BF16) for head in range(here)]
-    spread = (
-        (iota((columns, columns), 0) // QUERIES == iota((columns, columns), 1) // 64)
-        .astype(F32)
-        .astype(BF16)
-    )
-
-    in_events.wait()
-    for copies in in_w[1:]:
-        for copy in copies:
-            copy.start()
-    high, low = split(mm(place, rows_ref[0:length, :]))
-    rows_ref[length : length + 2 * users, :] = high
-    rows_ref[length + 2 * users :, :] = low
-
-    def store(step, part, means):
-        for sub in range(columns // 128):
-            group = step * (columns // 128) + sub
-            for rank in range(2):
-                out_ref[
-                    pl.ds(group * users * PARTS + part * 2 + rank, users, stride=PARTS), :
-                ] = means[rank * users : (rank + 1) * users, sub * 128 : (sub + 1) * 128]
+    spread = same_head(columns)
+
+    def put(group, part, rows):
+        for rank in range(2):
+            send_ref[pl.ds(group * users * PARTS + part * 2 + rank, users, stride=PARTS), :] = rows[
+                rank
+            ]
 
     def project(step):
-        for at in range(0, length, 256):
-            chunk = rows_ref[at : at + 256, :]
-            query_ref[step, at : at + 256, :] = mm(chunk, w_ref[step * 3]).astype(BF16)
-        for part, target in ((1, key_ref), (2, value_ref)):
+        for part, target in enumerate((query_ref, key_ref, value_ref)):
             for at in range(0, length, 256):
-                chunk = rows_ref[at : at + 256, :]
-                target[step, at : at + 256, :] = mm(chunk, w_ref[step * 3 + part]).astype(BF16)
-            extra = mm(rows_ref[length:, :], w_ref[step * 3 + part])
-            store(step, part, (extra[: 2 * users] + extra[2 * users :]) * inverse)
+                rows = rows_ref[at : at + 256, :]
+                target[step, at : at + 256, :] = mm(rows, w_ref[step * 3 + part]).astype(BF16)
+
+    def average(step):
+        means = []
+        for part in (1, 2):
+            both = mm(rows_ref[length:, :], w_ref[step * 3 + part])
+            mean = (both[: 2 * users] + both[2 * users :]) * inverse
+            keep_ref[
+                2 * part * users : 2 * (part + 1) * users, step * columns : (step + 1) * columns
+            ] = mean
+            means.append(mean)
+        for sub in range(subs):
+            group = step * subs + sub
+            key, later_key, value, later_value = [
+                mean[rank * users : (rank + 1) * users, sub * 128 : (sub + 1) * 128]
+                for mean in means
+                for rank in range(2)
+            ]
+            key = key * keep_ref[6 * users :, group * 128 : (group + 1) * 128]
+            x, y = key[:, 0:1], later_key[:, 0:1]
+            size = jnp.maximum(jnp.abs(x), jnp.abs(y))
+            some = size > 0.0
+            size = jnp.where(some, size, 1.0)
+            x, y = jnp.where(some, x / size, 1.0), y / size
+            norm = jnp.sqrt(x * x + y * y)
+            cosine = jnp.where(first, x / norm, 1.0)
+            sine = jnp.where(first, y / norm, 0.0)
+            turned = cosine * later_key - sine * key
+            total = gaps[0] + gaps[1]
+            put(group, 1, (cosine * key + sine * later_key, jnp.where(lane == 0, total, turned)))
+            put(
+                group,
+                2,
+                (cosine * value + sine * later_value, cosine * later_value - sine * value),
+            )
 
     def attend(step):
         offset = 0
@@ -186,55 +239,124 @@
     def finish(step):
         weight = mm(weight_ref[step].astype(BF16), spread)
         high, low = split(weight * value_ref[step].astype(F32))
-        store(step, 0, (mm(place, high) + mm(place, low)) * inverse)
-
+        mean = (mm(place, high) + mm(place, low)) * inverse
+        keep_ref[0 : 2 * users, step * columns : (step + 1) * columns] = mean
+        for sub in range(subs):
+            group = step * subs + sub
+            faded = mean[:, sub * 128 : (sub + 1) * 128] * fade_ref[
+                :, group * 128 : (group + 1) * 128
+            ]
+            put(group, 0, (faded[:users], faded[users:]))
+
+    in_events.wait()
+    for copies in in_w[1:]:
+        for copy in copies:
+            copy.start()
     for copy in in_w[0]:
         copy.wait()
+    high, low = split(mm(place, rows_ref[0:length, :]))
+    rows_ref[length : length + 2 * users, :] = high
+    rows_ref[length + 2 * users :, :] = low
     project(0)
-    for copies in in_w[1:]:
+    for copies in in_w[1:2]:
         for copy in copies:
             copy.wait()
     project(1)
+    for copies in in_w[2:4]:
+        for copy in copies:
+            copy.wait()
     project(2)
+    attend(0)
     project(3)
-    attend(0)
     attend(1)
+    average(0)
+    average(1)
+    average(2)
+    average(3)
     attend(2)
     finish(0)
     finish(1)
+    out_keys.start()
+    out[0].start()
+    out[1].start()
     attend(3)
     finish(2)
     finish(3)
-
-
-def encode(events, w_qkv, patterns, owners, gaps, users, groups):
+    out_queries.start()
+    out[2].start()
+    out[3].start()
+    for copy in [out_keys, out_queries] + out:
+        copy.wait()
+
+
+def encode(events, w_qkv, patterns, owners, gaps, rates, users, groups):
     length, width = events.shape
     columns = 256
     steps = width // columns
     window_rows = sum(size for _, _, size in windows(length))
-    rows = groups * users * PARTS
+    send = jax.ShapeDtypeStruct((groups * users * PARTS, 128), F32)
+    keep = jax.ShapeDtypeStruct((7 * users, width), F32)
     return pl.pallas_call(
         functools.partial(encode_kernel, users, groups),
-        in_specs=[pl.BlockSpec(memory_space=pl.ANY)] * 5,
-        out_shape=jax.ShapeDtypeStruct((rows, 128), F32),
+        in_specs=[pl.BlockSpec(memory_space=pl.ANY)] * 6,
+        out_specs=[pl.BlockSpec(memory_space=pl.ANY)] * 2,
+        out_shape=[send, keep],
         scratch_shapes=[
+            pltpu.VMEM(send.shape, F32),
+            pltpu.VMEM(keep.shape, F32),
+            pltpu.VMEM((2 * users, width), F32),
             pltpu.VMEM((length + 4 * users, width), BF16),
             pltpu.VMEM((3 * steps, width, columns), BF16),
             pltpu.VMEM((1, length), jnp.int32),
             pltpu.VMEM((1, SPP), jnp.int32),
             pltpu.VMEM((1, SPP), jnp.int32),
+            pltpu.SMEM(rates.shape, F32),
             pltpu.VMEM((window_rows, 128), F32),
             pltpu.VMEM((steps, length, columns), BF16),
             pltpu.VMEM((steps, length, columns), BF16),
             pltpu.VMEM((steps, length, columns), BF16),
             pltpu.VMEM((steps, length, columns), F32),
-            pltpu.SemaphoreType.DMA((3,)),
+            pltpu.SemaphoreType.DMA((4,)),
             pltpu.SemaphoreType.DMA,
             pltpu.SemaphoreType.DMA((3 * steps,)),
+            pltpu.SemaphoreType.DMA((steps + 2,)),
         ],
         compiler_params=pltpu.CompilerParams(vmem_limit_bytes=60 * 1024 * 1024),
         name="encode",
-    )(events, w_qkv, patterns, owners, gaps)
+    )(events, w_qkv, patterns, owners, gaps, rates)
+
+
+def within_kernel(users, keep_ref, out_ref):
+    query, later_query, key, later_key, value, later_value, fade = [
+        keep_ref[n * users : (n + 1) * users, :] for n in range(7)
+    ]
+    products = jnp.concatenate([query * key, later_query * key, later_query * later_key], axis=0)
+    columns = 256
+    spread = same_head(columns)
+    for at in range(0, products.shape[1], columns):
+        here = slice(at, at + columns)
+        part = products[:, here]
+        high = part.astype(BF16)
+        middle, low = split(part - high.astype(F32))
+        dots = mm(high, spread) + (mm(middle, spread) + mm(low, spread))
+        out_ref[:users, here] = dots[:users] * value[:, here]
+        out_ref[users:, here] = (
+            fade[:, here] * dots[users : 2 * users] * value[:, here]
+            + dots[2 * users :] * later_value[:, here]
+        )
+
+
+def within(keep, users):
+    width = keep.shape[1]
+    return pl.pallas_call(
+        functools.partial(within_kernel, users),
+        out_shape=jax.ShapeDtypeStruct((2 * users, width), F32),
+        compiler_params=pltpu.CompilerParams(vmem_limit_bytes=16 * 1024 * 1024),
+        cost_estimate=pl.CostEstimate(
+            flops=2 * 9 * users * width * 256, bytes_accessed=9 * users * width * 4, transcendentals=0
+        ),
+        name="within",
+    )(keep)
 
 
 def recur_kernel(packs, rates_hbm, rows_ref, prior_hbm, out_ref, rates_ref, prior_ref, sem):
@@ -244,27 +366,26 @@
     in_rates.start()
     in_prior.start()
     half = packs // 2
-    rows = 2 * packs
     load = lambda part, late: rows_ref[pl.ds(late * half * PARTS + part, half, stride=PARTS), :]
-    both = lambda part: jnp.concatenate(
-        [load(part + rank, late) for late in range(2) for rank in range(2)], axis=0
-    )
-    first = iota((1, 128), 1) < 64
-
-    def time(dim):
-        n = iota((rows, rows), dim)
-        return 2 * (n // packs * half + n % half) + n % packs // half
-
-    gap = []
+    both = lambda part: [load(part + rank, late) for late in range(2) for rank in range(2)]
+    lane = iota((1, 128), 1)
+    first = lane < 64
+
+    keys = both(2)
+    gap = jnp.concatenate([jnp.broadcast_to(keys[n][:, 0:1], (half, 128)) for n in (1, 3)], axis=0)
+    reached = (iota((packs, packs), 0) >= iota((packs, packs), 1)).astype(F32).astype(BF16)
+    ended = mm(reached, gap.astype(BF16))
+    started = ended - gap
+    ended_row = ended.T[0:1, :]
+    earlier = iota((half, half), 0) > iota((half, half), 1)
+    since = {}
     for late in range(2):
-        stored = load(6, late)
-        turned = pltpu.roll(stored, 64, 1)
-        gap += [jnp.where(first, stored, turned), jnp.where(first, turned, stored)]
-    causal = time(0) >= time(1)
-    elapsed = mm(causal.astype(F32).astype(BF16), jnp.concatenate(gap, axis=0).astype(BF16))
-    since = jnp.where(causal, elapsed[:, 0:1] - elapsed.T[0:1, :], 1e30)
-
-    query, key, value = both(0), both(2), both(4)
+        for source in range(late + 1):
+            gone = started[late * half : (late + 1) * half] - ended_row[:, source * half : (source + 1) * half]
+            since[late, source] = jnp.where(earlier, gone, 1e30) if late == source else gone
+
+    keys = [jnp.where(lane == 0, 0.0, rows) if n % 2 else rows for n, rows in enumerate(keys)]
+    query, key, value = [jnp.concatenate(rows, axis=0) for rows in (both(0), keys, both(4))]
     turned_query, turned_key = pltpu.roll(query, 64, 1), pltpu.roll(key, 64, 1)
     value_high, value_low = split(value)
     value_both = jnp.concatenate([value_high, value_low], axis=1)
@@ -281,7 +402,9 @@
         mine = first if head == 0 else jnp.logical_not(first)
         q_high, q_low = pieces(jnp.where(mine, query, turned_query))
         k_high, k_low = pieces(jnp.where(mine, key, turned_key))
-        left = jnp.concatenate([jnp.where(first, q_high, q_low), jnp.where(first, q_high, 0.0)], axis=1)
+        left = jnp.concatenate(
+            [jnp.where(first, q_high, q_low), jnp.where(first, q_high, 0.0)], axis=1
+        )
         right = jnp.concatenate([k_high, jnp.where(first, k_low, 0.0)], axis=1)
         sides.append((left.astype(BF16), right.astype(BF16)))
 
@@ -303,11 +426,16 @@
         heads = []
         for head in range(2):
             left, right = sides[head]
-            scores = mm(left[mine], right[seen], NT) * jnp.exp(-rate[head] * since[mine, seen])
+            fades = []
+            for source in range(late + 1):
+                fades += [jnp.exp(-rate[head] * since[late, source])] * 2
+            fades = jnp.concatenate(fades, axis=1)
+            scores = mm(left[mine], right[seen], NT) * jnp.concatenate([fades, fades], axis=0)
             s_high, s_low = split(scores)
             wide = mm(s_high, value_both[seen])
             heads.append(wide[:, :128] + (wide[:, 128:] + mm(s_low, value_high[seen])))
-        f_high, f_low = split(query[mine] * jnp.exp(-lane_rate * elapsed[mine]))
+        fade = jnp.exp(-lane_rate * started[late * half : (late + 1) * half])
+        f_high, f_low = split(query[mine] * jnp.concatenate([fade, fade], axis=0))
         carried = mm(jnp.concatenate([f_high, f_low], axis=1), prior_twice) + mm(f_high, prior_low)
         result = jnp.where(first, heads[0], heads[1]) + carried
         for rank in range(2):
@@ -335,15 +463,18 @@
     )(rates, rows, prior)
 
 
-def pick_kernel(users, groups, owner_hbm, rows_ref, out_ref, owner_ref, sem):
+def pick_kernel(users, groups, owner_hbm, rows_ref, within_ref, out_ref, owner_ref, sem):
     in_owner = pltpu.make_async_copy(owner_hbm, owner_ref, sem)
     in_owner.start()
     in_owner.wait()
     slots = jnp.concatenate(slots_of(owner_ref[...], users), axis=0).astype(BF16)
-    mine = jnp.concatenate(
+    mine = within_ref[...] + jnp.concatenate(
         [
             jnp.concatenate(
-                [rows_ref[pl.ds(group * users * 2 + rank, users, stride=2), :] for rank in range(2)],
+                [
+                    rows_ref[pl.ds(group * users * 2 + rank, users, stride=2), :]
+                    for rank in range(2)
+                ],
                 axis=0,
             )
             for group in range(groups)
@@ -355,18 +486,19 @@
     out_ref[...] = mm(slots, high, TN) + (mm(slots, middle, TN) + mm(slots, low, TN))
 
 
-def pick(owners, rows, users, groups):
+def pick(owners, rows, inside, users, groups):
     return pl.pallas_call(
         functools.partial(pick_kernel, users, groups),
         in_specs=[
             pl.BlockSpec(memory_space=pl.ANY),
+            pl.BlockSpec(memory_space=pltpu.VMEM),
             pl.BlockSpec(memory_space=pltpu.VMEM),
         ],
         out_shape=jax.ShapeDtypeStruct((SPP, groups * 128), F32),
         scratch_shapes=[pltpu.VMEM((1, SPP), jnp.int32), pltpu.SemaphoreType.DMA],
         compiler_params=pltpu.CompilerParams(vmem_limit_bytes=16 * 1024 * 1024),
         name="pick",
-    )(owners, rows)
+    )(owners, rows, inside)
 
 
 def shards(events, w_qkv, patterns, owners, gaps, rates, prior_state):
@@ -374,15 +506,19 @@
     users = lax.axis_size("sess")
     packs = groups * users
     axes = ("hist", "sess")
-    send = encode(events[0, 0], w_qkv, patterns[0], owners[0], gaps[0], users, groups)
+    send, keep = encode(
+        events[0, 0], w_qkv, patterns[0], owners[0], gaps[0], rates, users, groups
+    )
     arrived = lax.all_to_all(
         send.reshape(packs, PARTS, 1, 128), axes, split_axis=0, concat_axis=0, tiled=True
     ).reshape(packs * PARTS, 128)
+    inside = within(keep, users)
+    arrived, inside = lax.optimization_barrier((arrived, inside))
     done = recur(rates, arrived, prior_state[0], packs)
     returned = lax.all_to_all(
         done.reshape(packs, 2, 128), axes, split_axis=0, concat_axis=0, tiled=True
     ).reshape(packs * 2, 128)
-    return pick(owners[0], returned, users, groups)[None, None]
+    return pick(owners[0], returned, inside, users, groups)[None, None]
 
 
 def solution(mesh):

time: 79.9 us -> 76.3 us (0.955)
  blocking collectives: 66.1 us -> 20.8 us
  waiting for transfers between devices: 0 us -> 25.2 us
  starting transfers between devices: 0 us -> 15.7 us
  local copies, waits for them, and re-layouts: 0.01 us -> 1.18 us
    all_to_all x1 -> x0, blocking collectives: 45.2 us -> none  [shards(): lax.all_to_all(send.reshape(packs, PARTS, 1, 128), axes, split_axis=0, co...]
    all_to_all x0 -> x1, waiting for transfers between devices: none -> 25.2 us  [shards(): lax.all_to_all(send.reshape(packs, PARTS, 1, 128), axes, split_axis=0, co...]
    all_to_all x0 -> x1, starting transfers between devices: none -> 15.7 us  [shards(): lax.all_to_all(send.reshape(packs, PARTS, 1, 128), axes, split_axis=0, co...]
    unnamed x6 -> x8, local copies, waits for them, and re-layouts: 0.01 us -> 1.18 us
  transfers between devices with their start and end apart: 0 -> 1, of which waited for: 0 -> 1; matrix products, arithmetic and copies ran while one was open for 0% -> 0% of each run, Pallas kernels for 0% -> 1%
where the time goes in v4:
time: 76.3 us; the launch traced here: 76.1 us
  waiting for transfers between devices  25.2 us (33%)
  blocking collectives  20.8 us (27%)
  starting transfers between devices  15.7 us (21%)
  Pallas kernels  13.2 us (17%)
  local copies, waits for them, and re-layouts  1.18 us (2%)
    all_to_all x1, waiting for transfers between devices, shards(): lax.all_to_all(send.reshape(packs, PARTS, 1, 128), axes, split_axis=0, co...  25.2 us
    all_to_all x1, blocking collectives, shards(): lax.all_to_all(done.reshape(packs, 2, 128), axes, split_axis=0, concat_ax...  20.8 us
    all_to_all x1, starting transfers between devices, shards(): lax.all_to_all(send.reshape(packs, PARTS, 1, 128), axes, split_axis=0, co...  15.7 us
    pallas_call x1, Pallas kernels, encode(): pl.pallas_call(functools.partial(encode_kernel, users, groups), in_specs=...  9.83 us
    pallas_call x1, Pallas kernels, recur(): pl.pallas_call(functools.partial(recur_kernel, packs), in_specs=[pl.Block...  1.89 us
  transfers between devices with their start and end apart: 1, of which 1 were waited for; matrix products, arithmetic and copies ran while one was open for 0% of the time, Pallas kernels for 1%

profile of v4, /device:TPU:1, one launch (start us, length us, event | category | flops | bytes accessed | tf_op | source)
XLA Modules:
  0.0 76.1 jit_solution(9662597893935339535)
XLA Ops:
  0.0 0.0 copy-start.3
  0.0 0.0 copy-start.2
  0.0 0.0 copy-start.1
  0.0 9.8 %encode.1 = (f32[1536,128]{1,0:T(8,128)}, f32[224,1024]{1,0:T(8,128)}) custom-call(bf16[512,1024]{1,0:T(8,128)(2,1)} %bitcast.16, bf16[1024,3072]{1,0:T(8,128)(2,1)} %w_hbm.1, s32[1,512]{1,0:T(1,128)} %bitcast.18, s32[1,32]{1,0:T(1,128)} %bitcast.14, s32[1,32]{1,0:T(1,128)} %bitcast.19, f32[16]{0:T(128)} %rates_hbm.3), custom_call_target="tpu_custom_call" | custom-call | tf_op jit(solution)/shard_map/encode/pallas_call | solution.py:299
  9.8 15.7 %all-to-all-start = ((f32[256,6,1,128]{3,2,1,0:T(1,128)}), f32[256,6,1,128]{3,2,1,0:T(1,128)S(1)}, u32[]{:S(2)}, u32[]{:S(2)}) async-start(f32[256,6,1,128]{3,2,1,0:T(1,128)} %bitcast.17), calls=%async_computation | async-start | bytes 1572864 | tf_op jit(solution)/shard_map/all_to_all | solution.py:512
  25.5 0.0 copy-start
  25.5 1.2 %copy-done = f32[224,1024]{1,0:T(8,128)S(1)} copy-done((f32[224,1024]{1,0:T(8,128)S(1)}, f32[224,1024]{1,0:T(8,128)}, u32[]{:S(2)}) %copy-start) | copy-done | bytes 917528
  26.7 0.4 within.1.within_ref
  27.1 25.2 %all-to-all-done = f32[256,6,1,128]{3,2,1,0:T(1,128)S(1)} async-done(((f32[256,6,1,128]{3,2,1,0:T(1,128)}), f32[256,6,1,128]{3,2,1,0:T(1,128)S(1)}, u32[]{:S(2)}, u32[]{:S(2)}) %all-to-all-start) | async-done | bytes 786464 | tf_op jit(solution)/shard_map/all_to_all | solution.py:512
  52.3 0.0 copy-done.2
  52.3 0.0 copy-done.1
  52.3 1.9 %recur.1 = f32[512,128]{1,0:T(8,128)S(1)} custom-call(f32[16]{0:T(128)S(1)} %copy-done.2, f32[1536,128]{1,0:T(8,128)S(1)} %bitcast.10, f32[16,64,64]{2,1,0:T(8,128)S(1)} %bitcast.13), custom_call_target="tpu_custom_call" | custom-call | tf_op jit(solution)/shard_map/recur/pallas_call | solution.py:448
  54.2 20.8 %all_to_all.10 = f32[256,2,128]{2,1,0:T(2,128)S(1)} all-to-all(f32[256,2,128]{2,1,0:T(2,128)S(1)} %bitcast.12), channel_id=1, replica_groups=mesh['sess'=32,'hist'=8] {'hist','sess'}, dimensions={0} | all-to-all | bytes 524288 | tf_op jit(solution)/shard_map/all_to_all | solution.py:518
  75.1 0.0 copy-done.3
  75.1 1.0 %pick.1 = f32[32,1024]{1,0:T(8,128)} custom-call(s32[1,32]{1,0:T(1,128)S(1)} %bitcast.15, f32[512,128]{1,0:T(8,128)S(1)} %bitcast.11, f32[64,1024]{1,0:T(8,128)S(1)} %within.1.within_ref), custom_call_target="tpu_custom_call" | custom-call | tf_op jit(solution)/shard_map/pick/pallas_call | solution.py:490
Async XLA Ops:
  0.0 75.1 %copy-start.3 = (s32[1,1,32]{2,1,0:T(1,128)S(1)}, s32[1,1,32]{2,1,0:T(1,128)}, u32[]{:S(2)}) copy-start(s32[1,1,32]{2,1,0:T(1,128)} %param.10) | copy-start | bytes 388
  0.0 52.3 %copy-start.2 = (f32[16]{0:T(128)S(1)}, f32[16]{0:T(128)}, u32[]{:S(2)}) copy-start(f32[16]{0:T(128)} %rates_hbm.3) | copy-start | bytes 196
  0.0 52.3 %copy-start.1 = (f32[1,16,64,64]{3,2,1,0:T(8,128)S(1)}, f32[1,16,64,64]{3,2,1,0:T(8,128)}, u32[]{:S(2)}) copy-start(f32[1,16,64,64]{3,2,1,0:T(8,128)} %param.13) | copy-start | bytes 786436
  9.8 42.5 %all-to-all-start = ((f32[256,6,1,128]{3,2,1,0:T(1,128)}), f32[256,6,1,128]{3,2,1,0:T(1,128)S(1)}, u32[]{:S(2)}, u32[]{:S(2)}) async-start(f32[256,6,1,128]{3,2,1,0:T(1,128)} %bitcast.17), calls=%async_computation | async-start | bytes 1572864 | tf_op jit(solution)/shard_map/all_to_all | solution.py:512
  25.5 1.2 %copy-start = (f32[224,1024]{1,0:T(8,128)S(1)}, f32[224,1024]{1,0:T(8,128)}, u32[]{:S(2)}) copy-start(f32[224,1024]{1,0:T(8,128)} %get-tuple-element.10.keep_ref) | copy-start | bytes 2752516

commit v5 on v4

--- a/solution.py
+++ b/solution.py
@@ -145,6 +145,9 @@
     counts = jnp.sum(place, axis=1, keepdims=True)
     place = place.astype(BF16)
     inverse = jnp.broadcast_to(1.0 / jnp.maximum(counts, 1.0), (2 * users, columns))
+    for copies in in_w[1:4]:
+        for copy in copies:
+            copy.start()
     ids = iota((SPP, 128), 0).astype(F32).astype(BF16)
     id_column = mm(members, ids, TN)
     id_row = pattern.astype(F32)
@@ -237,9 +240,13 @@
             reached = low + size
 
     def finish(step):
-        weight = mm(weight_ref[step].astype(BF16), spread)
-        high, low = split(weight * value_ref[step].astype(F32))
-        mean = (mm(place, high) + mm(place, low)) * inverse
+        mean = None
+        for at in range(0, length, 128):
+            weight = mm(weight_ref[step, at : at + 128, :].astype(BF16), spread)
+            high, low = split(weight * value_ref[step, at : at + 128, :].astype(F32))
+            some = mm(place[:, at : at + 128], high) + mm(place[:, at : at + 128], low)
+            mean = some if mean is None else mean + some
+        mean = mean * inverse
         keep_ref[0 : 2 * users, step * columns : (step + 1) * columns] = mean
         for sub in range(subs):
             group = step * subs + sub
@@ -249,9 +256,6 @@
             put(group, 0, (faded[:users], faded[users:]))
 
     in_events.wait()
-    for copies in in_w[1:]:
-        for copy in copies:
-            copy.start()
     for copy in in_w[0]:
         copy.wait()
     high, low = split(mm(place, rows_ref[0:length, :]))
@@ -265,26 +269,26 @@
     for copies in in_w[2:4]:
         for copy in copies:
             copy.wait()
+    attend(0)
+    average(0)
+    attend(1)
+    average(1)
     project(2)
-    attend(0)
+    attend(2)
+    average(2)
     project(3)
-    attend(1)
-    average(0)
-    average(1)
-    average(2)
+    attend(3)
     average(3)
-    attend(2)
     finish(0)
     finish(1)
     out_keys.start()
     out[0].start()
     out[1].start()
-    attend(3)
     finish(2)
+    out[2].start()
     finish(3)
+    out[3].start()
     out_queries.start()
-    out[2].start()
-    out[3].start()
     for copy in [out_keys, out_queries] + out:
         copy.wait()
 
@@ -326,11 +330,12 @@
     )(events, w_qkv, patterns, owners, gaps, rates)
 
 
-def within_kernel(users, keep_ref, out_ref):
+def within_kernel(users, owner_ref, keep_ref, out_ref, chosen_ref):
     query, later_query, key, later_key, value, later_value, fade = [
         keep_ref[n * users : (n + 1) * users, :] for n in range(7)
     ]
     products = jnp.concatenate([query * key, later_query * key, later_query * later_key], axis=0)
+    chosen_ref[...] = jnp.concatenate(slots_of(owner_ref[...], users), axis=0).T
     columns = 256
     spread = same_head(columns)
     for at in range(0, products.shape[1], columns):
@@ -346,25 +351,27 @@
         )
 
 
-def within(keep, users):
+def within(owners, keep, users):
     width = keep.shape[1]
     return pl.pallas_call(
         functools.partial(within_kernel, users),
-        out_shape=jax.ShapeDtypeStruct((2 * users, width), F32),
+        out_shape=[
+            jax.ShapeDtypeStruct((2 * users, width), F32),
+            jax.ShapeDtypeStruct((SPP, 2 * users), F32),
+        ],
         compiler_params=pltpu.CompilerParams(vmem_limit_bytes=16 * 1024 * 1024),
         cost_estimate=pl.CostEstimate(
             flops=2 * 9 * users * width * 256, bytes_accessed=9 * users * width * 4, transcendentals=0
         ),
         name="within",
-    )(keep)
-
-
-def recur_kernel(packs, rates_hbm, rows_ref, prior_hbm, out_ref, rates_ref, prior_ref, sem):
-    group = lax.axis_index("hist")
-    in_rates = pltpu.make_async_copy(rates_hbm, rates_ref, sem.at[0])
-    in_prior = pltpu.make_async_copy(prior_hbm.at[pl.ds(2 * group, 2)], prior_ref, sem.at[1])
+    )(owners, keep)
+
+
+def recur_kernel(packs, users, rates_hbm, rows_ref, prior_ref, out_ref, rates_ref, sem):
+    core = lax.axis_index("core")
+    group = 2 * lax.axis_index("chip") + core
+    in_rates = pltpu.make_async_copy(rates_hbm, rates_ref, sem)
     in_rates.start()
-    in_prior.start()
     half = packs // 2
     load = lambda part, late: rows_ref[pl.ds(late * half * PARTS + part, half, stride=PARTS), :]
     both = lambda part: [load(part + rank, late) for late in range(2) for rank in range(2)]
@@ -390,7 +397,6 @@
     value_high, value_low = split(value)
     value_both = jnp.concatenate([value_high, value_low], axis=1)
     in_rates.wait()
-    in_prior.wait()
     rate = [rates_ref[2 * group], rates_ref[2 * group + 1]]
 
     def pieces(x):
@@ -411,8 +417,8 @@
     empty = jnp.zeros((64, 64), F32)
     prior = jnp.concatenate(
         [
-            jnp.concatenate([prior_ref[0], empty], axis=1),
-            jnp.concatenate([empty, prior_ref[1]], axis=1),
+            jnp.concatenate([prior_ref[2 * group], empty], axis=1),
+            jnp.concatenate([empty, prior_ref[2 * group + 1]], axis=1),
         ],
         axis=0,
     )
@@ -438,99 +444,107 @@
         f_high, f_low = split(query[mine] * jnp.concatenate([fade, fade], axis=0))
         carried = mm(jnp.concatenate([f_high, f_low], axis=1), prior_twice) + mm(f_high, prior_low)
         result = jnp.where(first, heads[0], heads[1]) + carried
-        for rank in range(2):
-            out_ref[pl.ds(late * packs + rank, half, stride=2), :] = (
-                result[rank * half : (rank + 1) * half]
-            )
-
-
-def recur(rates, rows, prior, packs):
+        for at in range(0, half, users):
+            segment = (late * half + at) // users
+            other = core if segment % 2 == 0 else 1 - core
+            for rank in range(2):
+                row = segment // 2 * users * 4 + 2 * other + rank
+                out_ref[pl.ds(row, users, stride=4), :] = result[
+                    rank * half + at : rank * half + at + users
+                ]
+
+
+def recur(rates, rows, prior, packs, users):
     return pl.pallas_call(
-        functools.partial(recur_kernel, packs),
-        in_specs=[
-            pl.BlockSpec(memory_space=pl.ANY),
-            pl.BlockSpec(memory_space=pltpu.VMEM),
-            pl.BlockSpec(memory_space=pl.ANY),
-        ],
-        out_shape=jax.ShapeDtypeStruct((2 * packs, 128), F32),
-        scratch_shapes=[
-            pltpu.SMEM(rates.shape, F32),
-            pltpu.VMEM((2, 64, 64), F32),
-            pltpu.SemaphoreType.DMA((2,)),
-        ],
-        compiler_params=pltpu.CompilerParams(vmem_limit_bytes=40 * 1024 * 1024),
-        name="recur",
-    )(rates, rows, prior)
-
-
-def pick_kernel(users, groups, owner_hbm, rows_ref, within_ref, out_ref, owner_ref, sem):
-    in_owner = pltpu.make_async_copy(owner_hbm, owner_ref, sem)
-    in_owner.start()
-    in_owner.wait()
-    slots = jnp.concatenate(slots_of(owner_ref[...], users), axis=0).astype(BF16)
-    mine = within_ref[...] + jnp.concatenate(
-        [
-            jnp.concatenate(
-                [
-                    rows_ref[pl.ds(group * users * 2 + rank, users, stride=2), :]
-                    for rank in range(2)
-                ],
-                axis=0,
-            )
-            for group in range(groups)
-        ],
-        axis=1,
-    )
-    high = mine.astype(BF16)
-    middle, low = split(mine - high.astype(F32))
-    out_ref[...] = mm(slots, high, TN) + (mm(slots, middle, TN) + mm(slots, low, TN))
-
-
-def pick(owners, rows, inside, users, groups):
-    return pl.pallas_call(
-        functools.partial(pick_kernel, users, groups),
+        functools.partial(recur_kernel, packs, users),
         in_specs=[
             pl.BlockSpec(memory_space=pl.ANY),
             pl.BlockSpec(memory_space=pltpu.VMEM),
             pl.BlockSpec(memory_space=pltpu.VMEM),
         ],
+        out_shape=jax.ShapeDtypeStruct((2 * packs, 128), F32),
+        scratch_shapes=[pltpu.SMEM(rates.shape, F32), pltpu.SemaphoreType.DMA],
+        compiler_params=pltpu.CompilerParams(vmem_limit_bytes=40 * 1024 * 1024),
+        name="recur",
+    )(rates, rows, prior)
+
+
+def pick_kernel(users, groups, chosen_ref, rows_ref, other_ref, within_ref, out_ref):
+    core = lax.axis_index("core")
+    chosen = chosen_ref[...].astype(BF16)
+    mine = []
+    for group in range(groups):
+        chip = group // 2 * users
+        here = [rows_ref[pl.ds(chip * 4 + rank, users, stride=4), :] for rank in range(2)]
+        there = [other_ref[pl.ds(chip * 2 + rank, users, stride=2), :] for rank in range(2)]
+        here, there = [jnp.concatenate(rows, axis=0) for rows in (here, there)]
+        mine.append(jnp.where(core == group % 2, here, there))
+    mine = within_ref[...] + jnp.concatenate(mine, axis=1)
+    high = mine.astype(BF16)
+    middle, low = split(mine - high.astype(F32))
+    out_ref[...] = mm(chosen, high) + (mm(chosen, middle) + mm(chosen, low))
+
+
+def pick(chosen, rows, other, inside, users, groups):
+    return pl.pallas_call(
+        functools.partial(pick_kernel, users, groups),
+        in_specs=[pl.BlockSpec(memory_space=pltpu.VMEM)] * 4,
         out_shape=jax.ShapeDtypeStruct((SPP, groups * 128), F32),
-        scratch_shapes=[pltpu.VMEM((1, SPP), jnp.int32), pltpu.SemaphoreType.DMA],
         compiler_params=pltpu.CompilerParams(vmem_limit_bytes=16 * 1024 * 1024),
         name="pick",
-    )(owners, rows, inside)
+    )(chosen, rows, other, inside)
 
 
 def shards(events, w_qkv, patterns, owners, gaps, rates, prior_state):
-    groups = lax.axis_size("hist")
+    chips = lax.axis_size("chip")
+    groups = 2 * chips
     users = lax.axis_size("sess")
     packs = groups * users
-    axes = ("hist", "sess")
     send, keep = encode(
         events[0, 0], w_qkv, patterns[0], owners[0], gaps[0], rates, users, groups
     )
     arrived = lax.all_to_all(
-        send.reshape(packs, PARTS, 1, 128), axes, split_axis=0, concat_axis=0, tiled=True
+        send.reshape(packs, PARTS, 1, 128),
+        ("chip", "core", "sess"),
+        split_axis=0,
+        concat_axis=0,
+        tiled=True,
     ).reshape(packs * PARTS, 128)
-    inside = within(keep, users)
-    arrived, inside = lax.optimization_barrier((arrived, inside))
-    done = recur(rates, arrived, prior_state[0], packs)
+    inside, chosen = within(owners[0], keep, users)
+    arrived, inside, chosen = lax.optimization_barrier((arrived, inside, chosen))
+    done = recur(rates, arrived, prior_state[0], packs, users)
     returned = lax.all_to_all(
-        done.reshape(packs, 2, 128), axes, split_axis=0, concat_axis=0, tiled=True
-    ).reshape(packs * 2, 128)
-    return pick(owners[0], returned, inside, users, groups)[None, None]
+        done.reshape(chips * users, 4, 128), ("chip", "sess"), split_axis=0, concat_axis=0, tiled=True
+    )
+    other = lax.ppermute(returned[:, 2:], "core", [(0, 1), (1, 0)])
+    return pick(
+        chosen,
+        returned.reshape(packs * 2, 128),
+        other.reshape(packs, 128),
+        inside,
+        users,
+        groups,
+    )[None, None]
 
 
 def solution(mesh):
+    sess, hist = mesh.shape["sess"], mesh.shape["hist"]
+    devices = mesh.devices if mesh.axis_names[0] == "sess" else mesh.devices.T
+    split_mesh = jax.sharding.Mesh(devices.reshape(sess, hist // 2, 2), ("sess", "chip", "core"))
+    segment = ("chip", "core")
     placed = (
-        P("hist", "sess", None, None),
+        P(segment, "sess", None, None),
         P(),
-        P("hist", "sess", None),
-        P("hist", "sess", None),
-        P("hist", "sess", None),
+        P(segment, "sess", None),
+        P(segment, "sess", None),
+        P(segment, "sess", None),
         P(),
         P("sess", None, None, None),
     )
     return jax.shard_map(
-        shards, mesh=mesh, in_specs=placed, out_specs=P("hist", "sess", None, None), check_vma=False
-    )
+        shards,
+        mesh=split_mesh,
+        in_specs=placed,
+        out_specs=P(segment, "sess", None, None),
+        check_vma=False,
+    )

time: 76.3 us -> 77.8 us (1.020)
  starting transfers between devices: 15.7 us -> 18.3 us
  blocking collectives: 20.8 us -> 19 us
  waiting for transfers between devices: 25.2 us -> 26.2 us
    ppermute x0 -> x1, starting transfers between devices: none -> 2.66 us  [shards(): other = lax.ppermute(returned[:, 2:], 'core', [(0, 1), (1, 0)])]
    all_to_all x1, blocking collectives: 20.8 us -> 19 us  [shards(): lax.all_to_all(done.reshape(chips * users, 4, 128), ('chip', 'sess'), spl...]
    ppermute x0 -> x1, waiting for transfers between devices: none -> 0.99 us  [shards(): other = lax.ppermute(returned[:, 2:], 'core', [(0, 1), (1, 0)])]
  transfers between devices with their start and end apart: 1 -> 2, of which waited for: 1 -> 2; matrix products, arithmetic and copies ran while one was open for 0% -> 0% of each run, Pallas kernels for 1% -> 1%
where the time goes in v5:
time: 77.8 us; the launch traced here: 77.6 us
  waiting for transfers between devices  26.2 us (34%)
  blocking collectives  19 us (24%)
  starting transfers between devices  18.3 us (24%)
  Pallas kernels  12.9 us (17%)
  local copies, waits for them, and re-layouts  1.25 us (2%)
    all_to_all x1, waiting for transfers between devices, shards(): lax.all_to_all(send.reshape(packs, PARTS, 1, 128), ('chip', 'core', 'sess...  25.2 us
    all_to_all x1, blocking collectives, shards(): lax.all_to_all(done.reshape(chips * users, 4, 128), ('chip', 'sess'), spl...  19 us
    all_to_all x1, starting transfers between devices, shards(): lax.all_to_all(send.reshape(packs, PARTS, 1, 128), ('chip', 'core', 'sess...  15.7 us
    pallas_call x1, Pallas kernels, encode(): pl.pallas_call(functools.partial(encode_kernel, users, groups), in_specs=...  9.67 us
    ppermute x1, starting transfers between devices, shards(): other = lax.ppermute(returned[:, 2:], 'core', [(0, 1), (1, 0)])  2.66 us
    pallas_call x1, Pallas kernels, recur(): pl.pallas_call(functools.partial(recur_kernel, packs, users), in_specs=[p...  1.89 us
  transfers between devices with their start and end apart: 2, of which 2 were waited for; matrix products, arithmetic and copies ran while one was open for 0% of the time, Pallas kernels for 1%

profile of v5, /device:TPU:1, one launch (start us, length us, event | category | flops | bytes accessed | tf_op | source)
XLA Modules:
  0.0 77.6 jit_solution(8445657045210837755)
XLA Ops:
  0.0 0.0 copy-start.2
  0.0 0.0 copy-start.3
  0.0 0.0 copy-start.1
  0.0 9.7 %encode.1 = (f32[1536,128]{1,0:T(8,128)}, f32[224,1024]{1,0:T(8,128)}) custom-call(bf16[512,1024]{1,0:T(8,128)(2,1)} %bitcast.18, bf16[1024,3072]{1,0:T(8,128)(2,1)} %w_hbm.1, s32[1,512]{1,0:T(1,128)} %bitcast.20, s32[1,32]{1,0:T(1,128)} %bitcast.16, s32[1,32]{1,0:T(1,128)} %bitcast.21, f32[16]{0:T(128)} %rates_hbm.3), custom_call_target="tpu_custom_call" | custom-call | tf_op jit(solution)/shard_map/encode/pallas_call | solution.py:303
  9.7 15.7 %all-to-all-start = ((f32[256,6,1,128]{3,2,1,0:T(1,128)}), f32[256,6,1,128]{3,2,1,0:T(1,128)S(1)}, u32[]{:S(2)}, u32[]{:S(2)}) async-start(f32[256,6,1,128]{3,2,1,0:T(1,128)} %bitcast.19), calls=%async_computation | async-start | bytes 1572864 | tf_op jit(solution)/shard_map/all_to_all | solution.py:506
  25.4 0.0 copy-done.2
  25.4 0.0 copy-start
  25.4 1.2 %copy-done = f32[224,1024]{1,0:T(8,128)S(1)} copy-done((f32[224,1024]{1,0:T(8,128)S(1)}, f32[224,1024]{1,0:T(8,128)}, u32[]{:S(2)}) %copy-start) | copy-done | bytes 917528
  26.5 0.4 within.1
  26.9 25.2 %all-to-all-done = f32[256,6,1,128]{3,2,1,0:T(1,128)S(1)} async-done(((f32[256,6,1,128]{3,2,1,0:T(1,128)}), f32[256,6,1,128]{3,2,1,0:T(1,128)S(1)}, u32[]{:S(2)}, u32[]{:S(2)}) %all-to-all-start) | async-done | bytes 786464 | tf_op jit(solution)/shard_map/all_to_all | solution.py:506
  52.1 0.0 copy-done.3
  52.1 0.0 copy-done.1
  52.1 1.9 %recur.1 = f32[512,128]{1,0:T(8,128)S(1)} custom-call(f32[16]{0:T(128)S(1)} %copy-done.3, f32[1536,128]{1,0:T(8,128)S(1)} %bitcast.11, f32[16,64,64]{2,1,0:T(8,128)S(1)} %bitcast.14), custom_call_target="tpu_custom_call" | custom-call | tf_op jit(solution)/shard_map/recur/pallas_call | solution.py:458
  54.0 19.0 %all_to_all.10 = f32[128,4,128]{2,1,0:T(4,128)S(1)} all-to-all(f32[128,4,128]{2,1,0:T(4,128)S(1)} %bitcast.13), channel_id=1, replica_groups=mesh['sess'=32,'chip'=4,'core'=2] {'chip','sess'}, dimensions={0} | all-to-all | bytes 524288 | tf_op jit(solution)/shard_map/all_to_all | solution.py:516
  73.0 0.1 slice.4
  73.1 2.7 %collective-permute-start = (f32[128,2,128]{2,1,0:T(2,128)S(1)}, f32[128,2,128]{2,1,0:T(2,128)S(1)}, u32[]{:S(2)}, u32[]{:S(2)}) collective-permute-start(f32[128,2,128]{2,1,0:T(2,128)S(1)} %slice.4), channel_id=1, source_target_pairs={{0,1},{1,0},{2,3},{3,2},{4,5},{5,4},{6,7},{7,6},{8,9},{9,8},{10,11... | collective-permute-start | bytes 393224 | tf_op jit(solution)/shard_map/ppermute | solution.py:519
  75.7 1.0 %collective-permute-done = f32[128,2,128]{2,1,0:T(2,128)S(1)} collective-permute-done((f32[128,2,128]{2,1,0:T(2,128)S(1)}, f32[128,2,128]{2,1,0:T(2,128)S(1)}, u32[]{:S(2)}, u32[]{:S(2)}) %collective-permute-start) | collective-permute-done | bytes 131104 | tf_op jit(solution)/shard_map/ppermute | solution.py:519
  76.7 0.9 %pick.1 = f32[32,1024]{1,0:T(8,128)} custom-call(f32[32,64]{1,0:T(8,128)S(1)} %get-tuple-element.16.chosen_ref, f32[512,128]{1,0:T(8,128)S(1)} %bitcast.12, f32[256,128]{1,0:T(8,128)S(1)} %bitcast.15, f32[64,1024]{1,0:T(8,128)S(1)} %get-tuple-element.18.within_ref), custom_call_target="tpu_custom_call" | custom-call | tf_op jit(solution)/shard_map/pick/pallas_call | solution.py:489
Async XLA Ops:
  0.0 25.4 %copy-start.2 = (s32[1,1,32]{2,1,0:T(1,128)S(1)}, s32[1,1,32]{2,1,0:T(1,128)}, u32[]{:S(2)}) copy-start(s32[1,1,32]{2,1,0:T(1,128)} %param.10) | copy-start | bytes 388
  0.0 52.1 %copy-start.3 = (f32[16]{0:T(128)S(1)}, f32[16]{0:T(128)}, u32[]{:S(2)}) copy-start(f32[16]{0:T(128)} %rates_hbm.3) | copy-start | bytes 196
  0.0 52.1 %copy-start.1 = (f32[1,16,64,64]{3,2,1,0:T(8,128)S(1)}, f32[1,16,64,64]{3,2,1,0:T(8,128)}, u32[]{:S(2)}) copy-start(f32[1,16,64,64]{3,2,1,0:T(8,128)} %param.13) | copy-start | bytes 786436
  9.7 42.4 %all-to-all-start = ((f32[256,6,1,128]{3,2,1,0:T(1,128)}), f32[256,6,1,128]{3,2,1,0:T(1,128)S(1)}, u32[]{:S(2)}, u32[]{:S(2)}) async-start(f32[256,6,1,128]{3,2,1,0:T(1,128)} %bitcast.19), calls=%async_computation | async-start | bytes 1572864 | tf_op jit(solution)/shard_map/all_to_all | solution.py:506
  25.4 1.2 %copy-start = (f32[224,1024]{1,0:T(8,128)S(1)}, f32[224,1024]{1,0:T(8,128)}, u32[]{:S(2)}) copy-start(f32[224,1024]{1,0:T(8,128)} %get-tuple-element.13.keep_ref) | copy-start | bytes 2752516
  73.1 3.6 %collective-permute-start = (f32[128,2,128]{2,1,0:T(2,128)S(1)}, f32[128,2,128]{2,1,0:T(2,128)S(1)}, u32[]{:S(2)}, u32[]{:S(2)}) collective-permute-start(f32[128,2,128]{2,1,0:T(2,128)S(1)} %slice.4), channel_id=1, source_target_pairs={{0,1},{1,0},{2,3},{3,2},{4,5},{5,4},{6,7},{7,6},{8,9},{9,8},{10,11... | collective-permute-start | bytes 393224 | tf_op jit(solution)/shard_map/ppermute | solution.py:519

commit v6 on v4

--- a/solution.py
+++ b/solution.py
@@ -145,6 +145,9 @@
     counts = jnp.sum(place, axis=1, keepdims=True)
     place = place.astype(BF16)
     inverse = jnp.broadcast_to(1.0 / jnp.maximum(counts, 1.0), (2 * users, columns))
+    for copies in in_w[1:4]:
+        for copy in copies:
+            copy.start()
     ids = iota((SPP, 128), 0).astype(F32).astype(BF16)
     id_column = mm(members, ids, TN)
     id_row = pattern.astype(F32)
@@ -237,9 +240,13 @@
             reached = low + size
 
     def finish(step):
-        weight = mm(weight_ref[step].astype(BF16), spread)
-        high, low = split(weight * value_ref[step].astype(F32))
-        mean = (mm(place, high) + mm(place, low)) * inverse
+        mean = None
+        for at in range(0, length, 128):
+            weight = mm(weight_ref[step, at : at + 128, :].astype(BF16), spread)
+            high, low = split(weight * value_ref[step, at : at + 128, :].astype(F32))
+            some = mm(place[:, at : at + 128], high) + mm(place[:, at : at + 128], low)
+            mean = some if mean is None else mean + some
+        mean = mean * inverse
         keep_ref[0 : 2 * users, step * columns : (step + 1) * columns] = mean
         for sub in range(subs):
             group = step * subs + sub
@@ -249,9 +256,6 @@
             put(group, 0, (faded[:users], faded[users:]))
 
     in_events.wait()
-    for copies in in_w[1:]:
-        for copy in copies:
-            copy.start()
     for copy in in_w[0]:
         copy.wait()
     high, low = split(mm(place, rows_ref[0:length, :]))
@@ -265,26 +269,26 @@
     for copies in in_w[2:4]:
         for copy in copies:
             copy.wait()
+    attend(0)
+    average(0)
+    attend(1)
+    average(1)
     project(2)
-    attend(0)
+    attend(2)
+    average(2)
     project(3)
-    attend(1)
-    average(0)
-    average(1)
-    average(2)
+    attend(3)
     average(3)
-    attend(2)
     finish(0)
     finish(1)
     out_keys.start()
     out[0].start()
     out[1].start()
-    attend(3)
     finish(2)
+    out[2].start()
     finish(3)
+    out[3].start()
     out_queries.start()
-    out[2].start()
-    out[3].start()
     for copy in [out_keys, out_queries] + out:
         copy.wait()
 
@@ -326,11 +330,12 @@
     )(events, w_qkv, patterns, owners, gaps, rates)
 
 
-def within_kernel(users, keep_ref, out_ref):
+def within_kernel(users, owner_ref, keep_ref, out_ref, chosen_ref):
     query, later_query, key, later_key, value, later_value, fade = [
         keep_ref[n * users : (n + 1) * users, :] for n in range(7)
     ]
     products = jnp.concatenate([query * key, later_query * key, later_query * later_key], axis=0)
+    chosen_ref[...] = jnp.concatenate(slots_of(owner_ref[...], users), axis=0).T
     columns = 256
     spread = same_head(columns)
     for at in range(0, products.shape[1], columns):
@@ -346,25 +351,26 @@
         )
 
 
-def within(keep, users):
+def within(owners, keep, users):
     width = keep.shape[1]
     return pl.pallas_call(
         functools.partial(within_kernel, users),
-        out_shape=jax.ShapeDtypeStruct((2 * users, width), F32),
+        out_shape=[
+            jax.ShapeDtypeStruct((2 * users, width), F32),
+            jax.ShapeDtypeStruct((SPP, 2 * users), F32),
+        ],
         compiler_params=pltpu.CompilerParams(vmem_limit_bytes=16 * 1024 * 1024),
         cost_estimate=pl.CostEstimate(
             flops=2 * 9 * users * width * 256, bytes_accessed=9 * users * width * 4, transcendentals=0
         ),
         name="within",
-    )(keep)
-
-
-def recur_kernel(packs, rates_hbm, rows_ref, prior_hbm, out_ref, rates_ref, prior_ref, sem):
+    )(owners, keep)
+
+
+def recur_kernel(packs, rates_hbm, rows_ref, prior_ref, out_ref, rates_ref, sem):
     group = lax.axis_index("hist")
-    in_rates = pltpu.make_async_copy(rates_hbm, rates_ref, sem.at[0])
-    in_prior = pltpu.make_async_copy(prior_hbm.at[pl.ds(2 * group, 2)], prior_ref, sem.at[1])
+    in_rates = pltpu.make_async_copy(rates_hbm, rates_ref, sem)
     in_rates.start()
-    in_prior.start()
     half = packs // 2
     load = lambda part, late: rows_ref[pl.ds(late * half * PARTS + part, half, stride=PARTS), :]
     both = lambda part: [load(part + rank, late) for late in range(2) for rank in range(2)]
@@ -390,7 +396,6 @@
     value_high, value_low = split(value)
     value_both = jnp.concatenate([value_high, value_low], axis=1)
     in_rates.wait()
-    in_prior.wait()
     rate = [rates_ref[2 * group], rates_ref[2 * group + 1]]
 
     def pieces(x):
@@ -411,8 +416,8 @@
     empty = jnp.zeros((64, 64), F32)
     prior = jnp.concatenate(
         [
-            jnp.concatenate([prior_ref[0], empty], axis=1),
-            jnp.concatenate([empty, prior_ref[1]], axis=1),
+            jnp.concatenate([prior_ref[2 * group], empty], axis=1),
+            jnp.concatenate([empty, prior_ref[2 * group + 1]], axis=1),
         ],
         axis=0,
     )
@@ -450,24 +455,17 @@
         in_specs=[
             pl.BlockSpec(memory_space=pl.ANY),
             pl.BlockSpec(memory_space=pltpu.VMEM),
-            pl.BlockSpec(memory_space=pl.ANY),
+            pl.BlockSpec(memory_space=pltpu.VMEM),
         ],
         out_shape=jax.ShapeDtypeStruct((2 * packs, 128), F32),
-        scratch_shapes=[
-            pltpu.SMEM(rates.shape, F32),
-            pltpu.VMEM((2, 64, 64), F32),
-            pltpu.SemaphoreType.DMA((2,)),
-        ],
+        scratch_shapes=[pltpu.SMEM(rates.shape, F32), pltpu.SemaphoreType.DMA],
         compiler_params=pltpu.CompilerParams(vmem_limit_bytes=40 * 1024 * 1024),
         name="recur",
     )(rates, rows, prior)
 
 
-def pick_kernel(users, groups, owner_hbm, rows_ref, within_ref, out_ref, owner_ref, sem):
-    in_owner = pltpu.make_async_copy(owner_hbm, owner_ref, sem)
-    in_owner.start()
-    in_owner.wait()
-    slots = jnp.concatenate(slots_of(owner_ref[...], users), axis=0).astype(BF16)
+def pick_kernel(users, groups, chosen_ref, rows_ref, within_ref, out_ref):
+    chosen = chosen_ref[...].astype(BF16)
     mine = within_ref[...] + jnp.concatenate(
         [
             jnp.concatenate(
@@ -483,22 +481,21 @@
     )
     high = mine.astype(BF16)
     middle, low = split(mine - high.astype(F32))
-    out_ref[...] = mm(slots, high, TN) + (mm(slots, middle, TN) + mm(slots, low, TN))
-
-
-def pick(owners, rows, inside, users, groups):
+    out_ref[...] = mm(chosen, high) + (mm(chosen, middle) + mm(chosen, low))
+
+
+def pick(chosen, rows, inside, users, groups):
     return pl.pallas_call(
         functools.partial(pick_kernel, users, groups),
         in_specs=[
-            pl.BlockSpec(memory_space=pl.ANY),
+            pl.BlockSpec(memory_space=pltpu.VMEM),
             pl.BlockSpec(memory_space=pltpu.VMEM),
             pl.BlockSpec(memory_space=pltpu.VMEM),
         ],
         out_shape=jax.ShapeDtypeStruct((SPP, groups * 128), F32),
-        scratch_shapes=[pltpu.VMEM((1, SPP), jnp.int32), pltpu.SemaphoreType.DMA],
         compiler_params=pltpu.CompilerParams(vmem_limit_bytes=16 * 1024 * 1024),
         name="pick",
-    )(owners, rows, inside)
+    )(chosen, rows, inside)
 
 
 def shards(events, w_qkv, patterns, owners, gaps, rates, prior_state):
@@ -512,13 +509,13 @@
     arrived = lax.all_to_all(
         send.reshape(packs, PARTS, 1, 128), axes, split_axis=0, concat_axis=0, tiled=True
     ).reshape(packs * PARTS, 128)
-    inside = within(keep, users)
-    arrived, inside = lax.optimization_barrier((arrived, inside))
+    inside, chosen = within(owners[0], keep, users)
+    arrived, inside, chosen = lax.optimization_barrier((arrived, inside, chosen))
     done = recur(rates, arrived, prior_state[0], packs)
     returned = lax.all_to_all(
         done.reshape(packs, 2, 128), axes, split_axis=0, concat_axis=0, tiled=True
     ).reshape(packs * 2, 128)
-    return pick(owners[0], returned, inside, users, groups)[None, None]
+    return pick(chosen, returned, inside, users, groups)[None, None]
 
 
 def solution(mesh):

time: 76.3 us -> 76 us (level)
  no operation moved by 1% of the time
where the time goes in v6:
time: 76 us; the launch traced here: 75.8 us
  waiting for transfers between devices  25.2 us (33%)
  blocking collectives  20.8 us (27%)
  starting transfers between devices  15.7 us (21%)
  Pallas kernels  12.9 us (17%)
  local copies, waits for them, and re-layouts  1.18 us (2%)
    all_to_all x1, waiting for transfers between devices, shards(): lax.all_to_all(send.reshape(packs, PARTS, 1, 128), axes, split_axis=0, co...  25.2 us
    all_to_all x1, blocking collectives, shards(): lax.all_to_all(done.reshape(packs, 2, 128), axes, split_axis=0, concat_ax...  20.8 us
    all_to_all x1, starting transfers between devices, shards(): lax.all_to_all(send.reshape(packs, PARTS, 1, 128), axes, split_axis=0, co...  15.7 us
    pallas_call x1, Pallas kernels, encode(): pl.pallas_call(functools.partial(encode_kernel, users, groups), in_specs=...  9.67 us
    pallas_call x1, Pallas kernels, recur(): pl.pallas_call(functools.partial(recur_kernel, packs), in_specs=[pl.Block...  1.89 us
  transfers between devices with their start and end apart: 1, of which 1 were waited for; matrix products, arithmetic and copies ran while one was open for 0% of the time, Pallas kernels for 1%

profile of v6, /device:TPU:1, one launch (start us, length us, event | category | flops | bytes accessed | tf_op | source)
XLA Modules:
  0.0 75.8 jit_solution(15714932227407165015)
XLA Ops:
  0.0 0.0 copy-start.2
  0.0 0.0 copy-start.3
  0.0 0.0 copy-start.1
  0.0 9.7 %encode.1 = (f32[1536,128]{1,0:T(8,128)}, f32[224,1024]{1,0:T(8,128)}) custom-call(bf16[512,1024]{1,0:T(8,128)(2,1)} %bitcast.16, bf16[1024,3072]{1,0:T(8,128)(2,1)} %w_hbm.1, s32[1,512]{1,0:T(1,128)} %bitcast.18, s32[1,32]{1,0:T(1,128)} %bitcast.14, s32[1,32]{1,0:T(1,128)} %bitcast.19, f32[16]{0:T(128)} %rates_hbm.3), custom_call_target="tpu_custom_call" | custom-call | tf_op jit(solution)/shard_map/encode/pallas_call | solution.py:303
  9.7 15.7 %all-to-all-start = ((f32[256,6,1,128]{3,2,1,0:T(1,128)}), f32[256,6,1,128]{3,2,1,0:T(1,128)S(1)}, u32[]{:S(2)}, u32[]{:S(2)}) async-start(f32[256,6,1,128]{3,2,1,0:T(1,128)} %bitcast.17), calls=%async_computation | async-start | bytes 1572864 | tf_op jit(solution)/shard_map/all_to_all | solution.py:509
  25.4 0.0 copy-done.2
  25.4 0.0 copy-start
  25.4 1.2 %copy-done = f32[224,1024]{1,0:T(8,128)S(1)} copy-done((f32[224,1024]{1,0:T(8,128)S(1)}, f32[224,1024]{1,0:T(8,128)}, u32[]{:S(2)}) %copy-start) | copy-done | bytes 917528
  26.5 0.4 within.1
  26.9 25.2 %all-to-all-done = f32[256,6,1,128]{3,2,1,0:T(1,128)S(1)} async-done(((f32[256,6,1,128]{3,2,1,0:T(1,128)}), f32[256,6,1,128]{3,2,1,0:T(1,128)S(1)}, u32[]{:S(2)}, u32[]{:S(2)}) %all-to-all-start) | async-done | bytes 786464 | tf_op jit(solution)/shard_map/all_to_all | solution.py:509
  52.1 0.0 copy-done.3
  52.1 0.0 copy-done.1
  52.1 1.9 %recur.1 = f32[512,128]{1,0:T(8,128)S(1)} custom-call(f32[16]{0:T(128)S(1)} %copy-done.3, f32[1536,128]{1,0:T(8,128)S(1)} %bitcast.10, f32[16,64,64]{2,1,0:T(8,128)S(1)} %bitcast.13), custom_call_target="tpu_custom_call" | custom-call | tf_op jit(solution)/shard_map/recur/pallas_call | solution.py:453
  54.0 20.8 %all_to_all.10 = f32[256,2,128]{2,1,0:T(2,128)S(1)} all-to-all(f32[256,2,128]{2,1,0:T(2,128)S(1)} %bitcast.12), channel_id=1, replica_groups=mesh['sess'=32,'hist'=8] {'hist','sess'}, dimensions={0} | all-to-all | bytes 524288 | tf_op jit(solution)/shard_map/all_to_all | solution.py:515
  74.9 0.9 %pick.1 = f32[32,1024]{1,0:T(8,128)} custom-call(f32[32,64]{1,0:T(8,128)S(1)} %get-tuple-element.16.chosen_ref, f32[512,128]{1,0:T(8,128)S(1)} %bitcast.11, f32[64,1024]{1,0:T(8,128)S(1)} %get-tuple-element.18.within_ref), custom_call_target="tpu_custom_call" | custom-call | tf_op jit(solution)/shard_map/pick/pallas_call | solution.py:488
Async XLA Ops:
  0.0 25.4 %copy-start.2 = (s32[1,1,32]{2,1,0:T(1,128)S(1)}, s32[1,1,32]{2,1,0:T(1,128)}, u32[]{:S(2)}) copy-start(s32[1,1,32]{2,1,0:T(1,128)} %param.10) | copy-start | bytes 388
  0.0 52.1 %copy-start.3 = (f32[16]{0:T(128)S(1)}, f32[16]{0:T(128)}, u32[]{:S(2)}) copy-start(f32[16]{0:T(128)} %rates_hbm.3) | copy-start | bytes 196
  0.0 52.1 %copy-start.1 = (f32[1,16,64,64]{3,2,1,0:T(8,128)S(1)}, f32[1,16,64,64]{3,2,1,0:T(8,128)}, u32[]{:S(2)}) copy-start(f32[1,16,64,64]{3,2,1,0:T(8,128)} %param.13) | copy-start | bytes 786436
  9.7 42.4 %all-to-all-start = ((f32[256,6,1,128]{3,2,1,0:T(1,128)}), f32[256,6,1,128]{3,2,1,0:T(1,128)S(1)}, u32[]{:S(2)}, u32[]{:S(2)}) async-start(f32[256,6,1,128]{3,2,1,0:T(1,128)} %bitcast.17), calls=%async_computation | async-start | bytes 1572864 | tf_op jit(solution)/shard_map/all_to_all | solution.py:509
  25.4 1.2 %copy-start = (f32[224,1024]{1,0:T(8,128)S(1)}, f32[224,1024]{1,0:T(8,128)}, u32[]{:S(2)}) copy-start(f32[224,1024]{1,0:T(8,128)} %get-tuple-element.13.keep_ref) | copy-start | bytes 2752516

commit v7 on v6

--- a/solution.py
+++ b/solution.py
@@ -425,24 +425,37 @@
     prior_twice = jnp.concatenate([prior_high, prior_high], axis=0)
     lane_rate = jnp.where(first, rate[0], rate[1])
 
-    for late in range(2):
-        mine = slice(late * packs, (late + 1) * packs)
-        seen = slice(0, (late + 1) * packs)
-        heads = []
+    total = [None, None]
+    for source in range(2):
+        seen = slice(source * packs, (source + 1) * packs)
+        later = range(source, 2)
+        scores = []
         for head in range(2):
             left, right = sides[head]
             fades = []
-            for source in range(late + 1):
-                fades += [jnp.exp(-rate[head] * since[late, source])] * 2
-            fades = jnp.concatenate(fades, axis=1)
-            scores = mm(left[mine], right[seen], NT) * jnp.concatenate([fades, fades], axis=0)
-            s_high, s_low = split(scores)
-            wide = mm(s_high, value_both[seen])
-            heads.append(wide[:, :128] + (wide[:, 128:] + mm(s_low, value_high[seen])))
+            for late in later:
+                fade = jnp.exp(-rate[head] * since[late, source])
+                fade = jnp.concatenate([fade, fade], axis=1)
+                fades += [fade, fade]
+            scores.append(
+                mm(left[source * packs :], right[seen], NT) * jnp.concatenate(fades, axis=0)
+            )
+        s_high, s_low = split(jnp.concatenate(scores, axis=1))
+        stacked = jnp.concatenate(
+            [jnp.where(first, value[seen], 0.0), jnp.where(first, 0.0, value[seen])], axis=0
+        )
+        v_high, v_low = split(stacked)
+        wide = mm(s_high, jnp.concatenate([v_high, v_low], axis=1))
+        part = wide[:, :128] + (wide[:, 128:] + mm(s_low, v_high))
+        for late in later:
+            some = part[(late - source) * packs : (late - source + 1) * packs]
+            total[late] = some if total[late] is None else total[late] + some
+    for late in range(2):
+        mine = slice(late * packs, (late + 1) * packs)
         fade = jnp.exp(-lane_rate * started[late * half : (late + 1) * half])
         f_high, f_low = split(query[mine] * jnp.concatenate([fade, fade], axis=0))
         carried = mm(jnp.concatenate([f_high, f_low], axis=1), prior_twice) + mm(f_high, prior_low)
-        result = jnp.where(first, heads[0], heads[1]) + carried
+        result = total[late] + carried
         for rank in range(2):
             out_ref[pl.ds(late * packs + rank, half, stride=2), :] = (
                 result[rank * half : (rank + 1) * half]

time: 76 us -> 75.7 us (level)
  no operation moved by 1% of the time
where the time goes in v7:
time: 75.7 us; the launch traced here: 75.5 us
  waiting for transfers between devices  25.2 us (33%)
  blocking collectives  20.8 us (27%)
  starting transfers between devices  15.7 us (21%)
  Pallas kernels  12.6 us (17%)
  local copies, waits for them, and re-layouts  1.18 us (2%)
    all_to_all x1, waiting for transfers between devices, shards(): lax.all_to_all(send.reshape(packs, PARTS, 1, 128), axes, split_axis=0, co...  25.2 us
    all_to_all x1, blocking collectives, shards(): lax.all_to_all(done.reshape(packs, 2, 128), axes, split_axis=0, concat_ax...  20.8 us
    all_to_all x1, starting transfers between devices, shards(): lax.all_to_all(send.reshape(packs, PARTS, 1, 128), axes, split_axis=0, co...  15.7 us
    pallas_call x1, Pallas kernels, encode(): pl.pallas_call(functools.partial(encode_kernel, users, groups), in_specs=...  9.67 us
    pallas_call x1, Pallas kernels, recur(): pl.pallas_call(functools.partial(recur_kernel, packs), in_specs=[pl.Block...  1.6 us
  transfers between devices with their start and end apart: 1, of which 1 were waited for; matrix products, arithmetic and copies ran while one was open for 0% of the time, Pallas kernels for 1%

profile of v7, /device:TPU:1, one launch (start us, length us, event | category | flops | bytes accessed | tf_op | source)
XLA Modules:
  0.0 75.5 jit_solution(18162102450856958765)
XLA Ops:
  0.0 0.0 copy-start.2
  0.0 0.0 copy-start.3
  0.0 0.0 copy-start.1
  0.0 9.7 %encode.1 = (f32[1536,128]{1,0:T(8,128)}, f32[224,1024]{1,0:T(8,128)}) custom-call(bf16[512,1024]{1,0:T(8,128)(2,1)} %bitcast.16, bf16[1024,3072]{1,0:T(8,128)(2,1)} %w_hbm.1, s32[1,512]{1,0:T(1,128)} %bitcast.18, s32[1,32]{1,0:T(1,128)} %bitcast.14, s32[1,32]{1,0:T(1,128)} %bitcast.19, f32[16]{0:T(128)} %rates_hbm.3), custom_call_target="tpu_custom_call" | custom-call | tf_op jit(solution)/shard_map/encode/pallas_call | solution.py:303
  9.7 15.7 %all-to-all-start = ((f32[256,6,1,128]{3,2,1,0:T(1,128)}), f32[256,6,1,128]{3,2,1,0:T(1,128)S(1)}, u32[]{:S(2)}, u32[]{:S(2)}) async-start(f32[256,6,1,128]{3,2,1,0:T(1,128)} %bitcast.17), calls=%async_computation | async-start | bytes 1572864 | tf_op jit(solution)/shard_map/all_to_all | solution.py:522
  25.4 0.0 copy-done.2
  25.4 0.0 copy-start
  25.4 1.2 %copy-done = f32[224,1024]{1,0:T(8,128)S(1)} copy-done((f32[224,1024]{1,0:T(8,128)S(1)}, f32[224,1024]{1,0:T(8,128)}, u32[]{:S(2)}) %copy-start) | copy-done | bytes 917528
  26.5 0.4 within.1
  26.9 25.2 %all-to-all-done = f32[256,6,1,128]{3,2,1,0:T(1,128)S(1)} async-done(((f32[256,6,1,128]{3,2,1,0:T(1,128)}), f32[256,6,1,128]{3,2,1,0:T(1,128)S(1)}, u32[]{:S(2)}, u32[]{:S(2)}) %all-to-all-start) | async-done | bytes 786464 | tf_op jit(solution)/shard_map/all_to_all | solution.py:522
  52.1 0.0 copy-done.3
  52.1 0.0 copy-done.1
  52.1 1.6 %recur.1 = f32[512,128]{1,0:T(8,128)S(1)} custom-call(f32[16]{0:T(128)S(1)} %copy-done.3, f32[1536,128]{1,0:T(8,128)S(1)} %bitcast.10, f32[16,64,64]{2,1,0:T(8,128)S(1)} %bitcast.13), custom_call_target="tpu_custom_call" | custom-call | tf_op jit(solution)/shard_map/recur/pallas_call | solution.py:466
  53.8 20.8 %all_to_all.10 = f32[256,2,128]{2,1,0:T(2,128)S(1)} all-to-all(f32[256,2,128]{2,1,0:T(2,128)S(1)} %bitcast.12), channel_id=1, replica_groups=mesh['sess'=32,'hist'=8] {'hist','sess'}, dimensions={0} | all-to-all | bytes 524288 | tf_op jit(solution)/shard_map/all_to_all | solution.py:528
  74.6 0.9 %pick.1 = f32[32,1024]{1,0:T(8,128)} custom-call(f32[32,64]{1,0:T(8,128)S(1)} %get-tuple-element.16.chosen_ref, f32[512,128]{1,0:T(8,128)S(1)} %bitcast.11, f32[64,1024]{1,0:T(8,128)S(1)} %get-tuple-element.18.within_ref), custom_call_target="tpu_custom_call" | custom-call | tf_op jit(solution)/shard_map/pick/pallas_call | solution.py:501
Async XLA Ops:
  0.0 25.4 %copy-start.2 = (s32[1,1,32]{2,1,0:T(1,128)S(1)}, s32[1,1,32]{2,1,0:T(1,128)}, u32[]{:S(2)}) copy-start(s32[1,1,32]{2,1,0:T(1,128)} %param.10) | copy-start | bytes 388
  0.0 52.1 %copy-start.3 = (f32[16]{0:T(128)S(1)}, f32[16]{0:T(128)}, u32[]{:S(2)}) copy-start(f32[16]{0:T(128)} %rates_hbm.3) | copy-start | bytes 196
  0.0 52.1 %copy-start.1 = (f32[1,16,64,64]{3,2,1,0:T(8,128)S(1)}, f32[1,16,64,64]{3,2,1,0:T(8,128)}, u32[]{:S(2)}) copy-start(f32[1,16,64,64]{3,2,1,0:T(8,128)} %param.13) | copy-start | bytes 786436
  9.7 42.4 %all-to-all-start = ((f32[256,6,1,128]{3,2,1,0:T(1,128)}), f32[256,6,1,128]{3,2,1,0:T(1,128)S(1)}, u32[]{:S(2)}, u32[]{:S(2)}) async-start(f32[256,6,1,128]{3,2,1,0:T(1,128)} %bitcast.17), calls=%async_computation | async-start | bytes 1572864 | tf_op jit(solution)/shard_map/all_to_all | solution.py:522
  25.4 1.2 %copy-start = (f32[224,1024]{1,0:T(8,128)S(1)}, f32[224,1024]{1,0:T(8,128)}, u32[]{:S(2)}) copy-start(f32[224,1024]{1,0:T(8,128)} %get-tuple-element.13.keep_ref) | copy-start | bytes 2752516
